TPU v7x, 256 devices: a whole 4x4x8 slice. The times are simulated.
256 devices in a mesh: lat: 32 (over y, z), chan: 8 (over x, core).
Axes of the slice: x: 4, y: 4, z: 8, core: 2. Of those that a mesh axis runs over, the one named last changes fastest.
Arguments:
- grid_in: bfloat16 [768, 1440, 256], P('lat', None, 'chan'), may hold values from -6 to 6
- pairing: int32 [384], replicated, may hold values from -1 to 359, as said below
- offsets: int32 [33], replicated, may hold values from 0 to 384, as said below
- legendre: bfloat16 [384, 721, 384], P('lat'), may hold values from -0.3125 to 0.3125
- degree_mix: bfloat16 [720, 256, 256], P(None, 'lat', 'chan'), may hold values from -0.375 to 0.375
- w_in: bfloat16 [256, 512], replicated, may hold values from -0.375 to 0.375
- w_out: bfloat16 [512, 256], replicated, may hold values from -0.25 to 0.25
Outputs:
- grid_out: bfloat16 [768, 1440, 256], P('lat', 'chan')
- spectrum: bfloat16 [384, 721, 2, 256], P('lat', None, None, 'chan')
Inputs may be any that keep to these rules, and one draw needn't show every extreme that they name: `pairing`: each value 0 to 359 stands in exactly one slot; every other slot holds -1; slot s belongs to lat device s // 12. offsets[0] = 0, offsets[32] = 384, offsets never fall, offsets[d] differs from d * 12 by at most 6, and some band holds exactly 24 latitudes.
All inputs are finite; a program needn't handle non-finite values.
Results may differ from a plain program's by a relative error of at most 0.013.
Values may be sent and summed in bfloat16 or wider, within the bound.
A program may use at most 256 MiB of HBM per device.

v0:
```python
import functools
import math

import jax
import jax.numpy as jnp
import ml_dtypes
import numpy as np
from jax import lax
from jax.experimental import pallas as pl
from jax.experimental.pallas import tpu as pltpu
from jax.sharding import Mesh
from jax.sharding import PartitionSpec as P

NLON = 1440
L = 720
KP = 721
SLOTS = 12
ROWS = 12
HALO = 6
CW = 32
NCH = 8
NY = 4
NZ = 8
NLATD = 32
CHUNK = 180
CHUNKP = 192
NPADDED = NCH * CHUNKP
JO = 12
JR = JO + 1
ENTRIES = 32 * JR
MROWS = 160
SG = 4
NSG = SLOTS // SG
EROWS = 2 * SG
F32 = jnp.float32
BF16 = jnp.bfloat16
VMEM_LIMIT = 56 * 1024 * 1024


def forward_table():
    n = np.arange(NLON, dtype=np.int64)
    m = np.arange(L, dtype=np.int64)
    ph = ((m[:, None] * n[None, :]) % NLON).astype(np.float32) * np.float32(2.0 * math.pi / NLON)
    f = np.float32(1.0 / math.sqrt(NLON))
    table = np.concatenate([np.cos(ph) * f, -np.sin(ph) * f], axis=0)
    return table.astype(ml_dtypes.bfloat16)


def inverse_table():
    n = np.arange(NLON, dtype=np.int64)
    m = np.arange(L, dtype=np.int64)
    ph = ((n[:, None] * m[None, :]) % NLON).astype(np.float32) * np.float32(2.0 * math.pi / NLON)
    f = np.float32(1.0 / math.sqrt(NLON))
    w = np.where(m == 0, 1.0, 2.0).astype(np.float32)[None, :] * f
    table = np.concatenate([np.cos(ph) * w, -np.sin(ph) * w], axis=1)
    padded = np.zeros((NCH, CHUNKP, 2 * L), np.float32)
    padded[:, :CHUNK] = table.reshape(NCH, CHUNK, 2 * L)
    return padded.reshape(NPADDED, 2 * L).astype(ml_dtypes.bfloat16)


def pad_rows():
    sel = np.zeros((NCH, CHUNKP, NLON), np.float32)
    for c in range(NCH):
        for i in range(CHUNK):
            sel[c, i, c * CHUNK + i] = 1.0
    return sel.reshape(NPADDED, NLON).astype(ml_dtypes.bfloat16)


def degree_order():
    sel = np.zeros((32, 2 * JO, L), np.float32)
    for o in range(L // 2 // JO):
        for jj in range(JO):
            j = o * JO + jj
            sel[o, jj, j] = 1.0
            sel[o, JO + jj, L - 1 - j] = 1.0
    return sel.reshape(32 * 2 * JO, L).astype(ml_dtypes.bfloat16)


def swap_table():
    sel = np.zeros((4, 4, CW, 4, 4, CW), np.float32)
    for q in range(4):
        for r in range(4):
            for c in range(CW):
                sel[q, r, c, r, q, c] = 1.0
    return sel.reshape(512, 512).astype(ml_dtypes.bfloat16)


def swap_mirror_table():
    base = swap_table().reshape(512, 4, 4, CW)
    return np.concatenate([base, base[:, :, [2, 3, 0, 1]]], axis=2).reshape(512, 1024)


def swap4(v, table):
    joined = jnp.concatenate([x.astype(BF16) for x in v], axis=1)
    out = jnp.dot(joined, table, preferred_element_type=F32)
    width = out.shape[1] // 4
    return [out[:, k * width : (k + 1) * width] for k in range(4)]


def pair_one_hots(base):
    ri = lax.broadcasted_iota(jnp.int32, (32 * JR, 1), 0)
    jj = ri // 32
    o = ri % 32
    j = JO * o + jj
    regular = (jj < JO) & (j < L // 2)
    extra = (jj == JO) & (base // JO == o)
    kx = jnp.where(regular, L - 1 - base - j, jnp.where(extra, L - base, -1))
    ky = jnp.where(regular, jnp.where(j >= base, j - base, L - j), -1)
    col = lax.broadcasted_iota(jnp.int32, (32 * JR, KP), 1)
    sx = jnp.where(col == kx, 1.0, 0.0).astype(BF16)
    sy = jnp.where(col == ky, 1.0, 0.0).astype(BF16)
    return sx, sy


def legendre_kernel(first_ref, inc_ref, leg_ref, swap_ref, out_ref, scr_f, scr_r, scr_o):
    group = pl.program_id(0)

    @pl.when(group == 0)
    def _():
        for k in range(6):
            scr_f[k] = inc_ref[:, k * 128 : k * 128 + 128].astype(F32)
        scr_o[...] = jnp.zeros_like(scr_o)

    row = lax.broadcasted_iota(jnp.int32, (ENTRIES, 128), 0)
    lane = lax.broadcasted_iota(jnp.int32, (ENTRIES, 128), 1)
    degree = JO * (row % 32) + row // 32
    for ss in range(SG):
        s = group * SG + ss
        t = [
            jnp.concatenate(
                [
                    scr_f.at[p * 3 + rg][pl.ds(side * SLOTS + s, 32, stride=24), :]
                    for rg in range(3)
                ],
                axis=0,
            )
            for side in range(2)
            for p in range(2)
        ]
        for r4, u in enumerate(swap4(t, swap_ref[...])):
            for rg in range(3):
                for k in range(2):
                    scr_r.at[ss * 2 + k][pl.ds(rg * 4 + r4, 32, stride=ROWS), :] = u[
                        rg * 32 : rg * 32 + 32, k * 128 : k * 128 + 128
                    ]
        right = jnp.concatenate([scr_r[ss * 2], scr_r[ss * 2 + 1]], axis=1).astype(BF16)
        both = jnp.dot(leg_ref[ss], right, preferred_element_type=F32)
        base = jnp.maximum(first_ref[s], 0)
        x = jnp.where(row < 32 * JO, both[:ENTRIES, :128], both[:ENTRIES, 128:])
        y = jnp.where(degree >= base, both[ENTRIES:, 128:], both[ENTRIES:, :128])
        q = jnp.where(lane < 64, x, y)
        for jj in range(JR):
            scr_o[pl.ds(s * JR + jj, 32, stride=MROWS), :] = q[jj * 32 : jj * 32 + 32]

    @pl.when(group == NSG - 1)
    def _():
        out_ref[...] = scr_o[...].astype(BF16)


def run_legendre(first, incoming, table):
    return pl.pallas_call(
        legendre_kernel,
        grid_spec=pltpu.PrefetchScalarGridSpec(
            num_scalar_prefetch=1,
            grid=(NSG,),
            in_specs=[
                pl.BlockSpec((NLATD * 24, 2 * ROWS * CW), lambda g, f: (0, 0)),
                pl.BlockSpec((SG, 2 * ENTRIES, NLATD * ROWS), lambda g, f: (g, 0, 0)),
                pl.BlockSpec((512, 1024), lambda g, f: (0, 0)),
            ],
            out_specs=pl.BlockSpec((32 * MROWS, 128), lambda g, f: (0, 0)),
            scratch_shapes=[
                pltpu.VMEM((6, NLATD * 24, 128), F32),
                pltpu.VMEM((2 * SG, NLATD * ROWS, 128), F32),
                pltpu.VMEM((32 * MROWS, 128), F32),
            ],
        ),
        out_shape=jax.ShapeDtypeStruct((32 * MROWS, 128), BF16),
        compiler_params=pltpu.CompilerParams(vmem_limit_bytes=VMEM_LIMIT),
        name="legendre_forward",
    )(first, incoming, table, jnp.asarray(swap_mirror_table()))


def weights_kernel(w_ref, swap_ref, out_ref, scr):
    for zz in range(2):
        unpack_one(w_ref, swap_ref, out_ref, scr, zz)


def unpack_one(w_ref, swap_ref, out_ref, scr, zz):
    for h in range(2):
        for ih in range(2):
            t = [
                jnp.concatenate(
                    [
                        w_ref[zz, y * 8 + h * 4 + c, :, ih * 128 : ih * 128 + 128].astype(F32)
                        for y in range(NY)
                    ],
                    axis=0,
                )
                for c in range(4)
            ]
            for i4, u in enumerate(swap4(t, swap_ref[...])):
                for y in range(NY):
                    scr.at[zz * 2 + h][pl.ds(y * 8 + ih * 4 + i4, 2 * JO, stride=32), :] = u[
                        y * 2 * JO : (y + 1) * 2 * JO
                    ]
    for h in range(2):
        out_ref[:, :, zz, :, h * 128 : h * 128 + 128] = scr[zz * 2 + h].astype(BF16).reshape(2 * JO, NY, 8, 128)


def run_weights(gathered):
    return pl.pallas_call(
        weights_kernel,
        grid=(NZ // 2,),
        in_specs=[
            pl.BlockSpec((2, 32, 2 * JO, 256), lambda z: (z, 0, 0, 0)),
            pl.BlockSpec((512, 512), lambda z: (0, 0)),
        ],
        out_specs=pl.BlockSpec((2 * JO, NY, 2, 8, 256), lambda z: (0, 0, z, 0, 0)),
        scratch_shapes=[pltpu.VMEM((4, 2 * JO * 32, 128), F32)],
        out_shape=jax.ShapeDtypeStruct((2 * JO, NY, NZ, 8, 256), BF16),
        cost_estimate=pl.CostEstimate(flops=4 * 10**9, bytes_accessed=6 * 10**6, transcendentals=0),
        compiler_params=pltpu.CompilerParams(vmem_limit_bytes=VMEM_LIMIT),
        name="unpack_weights",
    )(gathered, jnp.asarray(swap_table()))


VROWS = NY * MROWS


def mix_kernel(owner_ref, d_ref, w_ref, a_ref, swap_ref, out_ref, v, ex):
    for y in range(NY):
        for h in range(2):
            t = [d_ref[y * 8 + h * 4 + i] for i in range(4)]
            for q, u in enumerate(swap4(t, swap_ref[...])):
                v[h, q * VROWS + y * MROWS : q * VROWS + (y + 1) * MROWS, :] = u
    v[:, 4 * VROWS :, :] = jnp.zeros((2, v.shape[1] - 4 * VROWS, 128), F32)
    lane_a = a_ref[...]

    def rows(q, jj):
        return jnp.concatenate(
            [
                jnp.concatenate(
                    [v.at[h][pl.ds(start, 16, stride=JR), :] for h in range(2)], axis=1
                )
                for start in (q * VROWS + y * MROWS + jj for y in range(NY))
            ],
            axis=0,
        )

    extra = jnp.concatenate([rows(0, JO), rows(1, JO)], axis=0).astype(BF16)
    ex[...] = jnp.zeros_like(ex)
    owner = owner_ref[0]

    def put(q, jj, value):
        for y in range(NY):
            start = q * VROWS + y * MROWS + jj
            for h in range(2):
                v.at[h][pl.ds(start, SLOTS, stride=JR), :] = value[
                    y * 16 : y * 16 + SLOTS, h * 128 : h * 128 + 128
                ]

    for jj in range(JO):
        j = owner * JO + jj
        x = jnp.concatenate([rows(0, jj), rows(1, jj)], axis=0).astype(BF16)
        yv = jnp.concatenate([rows(2, jj), rows(3, jj)], axis=0).astype(BF16)
        upper = jnp.dot(
            jnp.concatenate([x, yv, extra], axis=0), w_ref[JO + jj], preferred_element_type=F32
        )
        lower = jnp.dot(yv, w_ref[jj], preferred_element_type=F32)
        ym = jnp.where(lane_a <= j, lower, upper[128:256])
        ex[...] += jnp.where(lane_a == j, upper[256:384], 0.0)
        put(0, jj, upper[0:64])
        put(1, jj, upper[64:128])
        put(2, jj, ym[0:64])
        put(3, jj, ym[64:128])
    put(0, JO, ex[0:64, :])
    put(1, JO, ex[64:128, :])
    for y in range(NY):
        for h in range(2):
            t = [
                v[h, q * VROWS + y * MROWS : q * VROWS + (y + 1) * MROWS, :]
                for q in range(4)
            ]
            for i, u in enumerate(swap4(t, swap_ref[...])):
                out_ref[y * 8 + h * 4 + i] = u.astype(BF16)


def run_mix(owner, coeffs, weights, lower_orders):
    return pl.pallas_call(
        mix_kernel,
        in_specs=[
            pl.BlockSpec(memory_space=pltpu.SMEM),
            pl.BlockSpec(memory_space=pltpu.VMEM),
            pl.BlockSpec(memory_space=pltpu.VMEM),
            pl.BlockSpec(memory_space=pltpu.VMEM),
            pl.BlockSpec(memory_space=pltpu.VMEM),
        ],
        out_specs=pl.BlockSpec(memory_space=pltpu.VMEM),
        scratch_shapes=[pltpu.VMEM((2, 4 * VROWS + 64, 128), F32), pltpu.VMEM((128, 256), F32)],
        out_shape=jax.ShapeDtypeStruct((32, MROWS, 128), BF16),
        compiler_params=pltpu.CompilerParams(vmem_limit_bytes=VMEM_LIMIT),
        name="mix_degrees",
    )(owner, coeffs, weights, lower_orders, jnp.asarray(swap_table()))


def inverse_kernel(
    first_ref, d_ref, turned_ref, swap_ref, spec_ref, home_ref,
    scr_f, scr_b, scr_e, entries, leaving, send_sem, recv_sem, local_sem,
):
    group = pl.program_id(0)
    me = own_index("lat")
    barrier = pltpu.get_barrier_semaphore()

    @pl.when(group == 0)
    def _():
        greet("lat", NLATD, barrier)
        scr_f[...] = d_ref[...].astype(F32)

    row = lax.broadcasted_iota(jnp.int32, (ENTRIES, 128), 0)
    left = lax.broadcasted_iota(jnp.int32, (ENTRIES, 128), 1) < 64
    degree = JO * (row % 32) + row // 32
    for ss in range(SG):
        s = group * SG + ss
        q = jnp.concatenate(
            [scr_f[pl.ds(s * JR + jj, 32, stride=MROWS), :] for jj in range(JR)], axis=0
        )
        entries[s] = q.astype(BF16)
        qs = pltpu.roll(q, 64, 1)
        base = jnp.maximum(first_ref[s], 0)
        x = jnp.where(row < 32 * JO, jnp.where(left, q, 0.0), jnp.where(left, 0.0, qs)).astype(BF16)
        y = jnp.where(degree >= base, jnp.where(left, qs, 0.0), jnp.where(left, 0.0, q)).astype(BF16)
        scr_b[ss] = jnp.dot(turned_ref[ss, 0], x, preferred_element_type=F32) + jnp.dot(
            turned_ref[ss, 1], y, preferred_element_type=F32
        )
        t = [
            jnp.concatenate(
                [scr_b.at[ss][pl.ds(rg * 4 + r4, 32, stride=ROWS), :] for rg in range(3)], axis=0
            )
            for r4 in range(4)
        ]
        for qi, u in enumerate(swap4(t, swap_ref[...])):
            for rg in range(3):
                scr_e.at[(qi % 2) * 3 + rg][pl.ds((qi // 2) * SG + ss, 32, stride=EROWS), :] = u[
                    rg * 32 : rg * 32 + 32
                ]
    for k in range(6):
        leaving[group, :, :, k * 128 : k * 128 + 128] = (
            scr_e[k].reshape(NLATD, EROWS, 128).astype(BF16)
        )

    @pl.when(group == 0)
    def _():
        pl.semaphore_wait(barrier, NLATD - 1)

    def send(g, k):
        peer = peer_of("lat", k, 1)
        return pltpu.make_async_remote_copy(
            src_ref=leaving.at[g, peer],
            dst_ref=home_ref.at[g, me],
            send_sem=send_sem.at[g, k],
            recv_sem=recv_sem.at[g, k],
            device_id=partner("lat", peer),
            device_id_type=pl.DeviceIdType.MESH,
        )

    def start(k, carry):
        send(group, k).start()
        return carry

    lax.fori_loop(1, NLATD, start, 0)
    pltpu.make_async_copy(leaving.at[group, me], home_ref.at[group, me], local_sem.at[group]).start()

    @pl.when(group == NSG - 1)
    def _():
        def pack(s, carry):
            sx, sy = pair_one_hots(jnp.maximum(first_ref[s], 0))
            qt = jnp.transpose(entries[s].astype(F32)).astype(BF16)
            spec_ref[s] = (
                jnp.dot(qt[:64], sx, preferred_element_type=F32)
                + jnp.dot(qt[64:], sy, preferred_element_type=F32)
            ).astype(BF16)
            return carry

        lax.fori_loop(0, SLOTS, pack, 0)
        for g in range(NSG):

            def finish(k, carry):
                send(g, k).wait_send()
                source = peer_of("lat", k, -1)
                pltpu.make_async_remote_copy(
                    src_ref=leaving.at[g, source],
                    dst_ref=home_ref.at[g, source],
                    send_sem=send_sem.at[g, k],
                    recv_sem=recv_sem.at[g, k],
                    device_id=partner("lat", source),
                    device_id_type=pl.DeviceIdType.MESH,
                ).wait_recv()
                return carry

            lax.fori_loop(1, NLATD, finish, 0)
            pltpu.make_async_copy(leaving.at[g, me], home_ref.at[g, me], local_sem.at[g]).wait()


def run_inverse(first, mixed, turned):
    return pl.pallas_call(
        inverse_kernel,
        grid=(NSG,),
        in_specs=[
            pl.BlockSpec(memory_space=pltpu.SMEM),
            pl.BlockSpec((32 * MROWS, 128), lambda g: (0, 0)),
            pl.BlockSpec((SG, 2, NLATD * ROWS, ENTRIES), lambda g: (g, 0, 0, 0)),
            pl.BlockSpec((512, 512), lambda g: (0, 0)),
        ],
        out_specs=[
            pl.BlockSpec((SLOTS, 2 * CW, KP), lambda g: (0, 0, 0)),
            pl.BlockSpec(memory_space=pl.ANY),
        ],
        scratch_shapes=[
            pltpu.VMEM((32 * MROWS, 128), F32),
            pltpu.VMEM((SG, NLATD * ROWS, 128), F32),
            pltpu.VMEM((6, NLATD * EROWS, 128), F32),
            pltpu.VMEM((SLOTS, ENTRIES, 128), BF16),
            pltpu.VMEM((NSG, NLATD, EROWS, 2 * ROWS * CW), BF16),
            pltpu.SemaphoreType.DMA((NSG, NLATD)),
            pltpu.SemaphoreType.DMA((NSG, NLATD)),
            pltpu.SemaphoreType.DMA((NSG,)),
        ],
        out_shape=[
            jax.ShapeDtypeStruct((SLOTS, 2 * CW, KP), BF16),
            jax.ShapeDtypeStruct((NSG, NLATD, EROWS, 2 * ROWS * CW), BF16),
        ],
        compiler_params=pltpu.CompilerParams(
            vmem_limit_bytes=VMEM_LIMIT, collective_id=3, has_side_effects=True
        ),
        name="legendre_inverse_home",
    )(first, mixed, turned, jnp.asarray(swap_table()))


PIECES = ((0, 4, 0), (4, 6, 4), (6, 8, 0), (8, 12, 2))


def tail_kernel(
    x_ref, w_in_ref, w_out_ref, swap_ref, own_ref, left_ref, right_ref,
    recv, res, v, send_sem, recv_sem, local_sem, halo_send, halo_recv, own_sem,
):
    me = own_index("chan")
    band = own_index("lat")
    rightward = lax.rem(band + 1, NLATD)
    leftward = lax.rem(band + NLATD - 1, NLATD)
    barrier = pltpu.get_barrier_semaphore()
    greet("chan", NCH, barrier)
    for neighbour in (leftward, rightward):
        pl.semaphore_signal(
            barrier, inc=1, device_id=partner("lat", neighbour), device_id_type=pl.DeviceIdType.MESH
        )

    def local(rg):
        at = pl.ds(rg * 128, 128)
        return pltpu.make_async_copy(x_ref.at[me, :, at], recv.at[me, :, at], local_sem.at[rg])

    for rg in range(3):
        local(rg).start()
    pl.semaphore_wait(barrier, NCH + 1)

    def copy(rg, k, sign):
        peer = peer_of("chan", k, sign)
        at = pl.ds(rg * 128, 128)
        return pltpu.make_async_remote_copy(
            src_ref=x_ref.at[peer, :, at],
            dst_ref=recv.at[me if sign == 1 else peer, :, at],
            send_sem=send_sem.at[rg, k],
            recv_sem=recv_sem.at[rg, k],
            device_id=partner("chan", peer),
            device_id_type=pl.DeviceIdType.MESH,
        )

    for rg in range(3):

        def start(k, carry):
            copy(rg, k, 1).start()
            return carry

        lax.fori_loop(1, NCH, start, 0)

    def halo(piece):
        first, last, place = PIECES[piece]
        there = right_ref if piece < 2 else left_ref
        return pltpu.make_async_remote_copy(
            src_ref=res.at[pl.ds(first, last - first)],
            dst_ref=there.at[pl.ds(place, last - first)],
            send_sem=halo_send.at[piece],
            recv_sem=halo_recv.at[piece],
            device_id=partner("lat", leftward if piece < 2 else rightward),
            device_id_type=pl.DeviceIdType.MESH,
        )

    for rg in range(3):

        def arrive(k, carry):
            copy(rg, k, -1).wait_recv()
            return carry

        lax.fori_loop(1, NCH, arrive, 0)
        local(rg).wait()
        for h in range(2):
            t = [recv[h * 4 + i, :, rg * 128 : rg * 128 + 128] for i in range(4)]
            for r4, u in enumerate(swap4(t, swap_ref[...])):
                v[r4 * CHUNKP : (r4 + 1) * CHUNKP, h * 128 : h * 128 + 128] = u
        values = v[...]
        centered = values - jnp.mean(values, axis=-1, keepdims=True)
        normed = (
            centered * lax.rsqrt(jnp.mean(centered * centered, axis=-1, keepdims=True) + 1e-05)
        ).astype(BF16)
        hidden = jax.nn.gelu(
            jnp.dot(normed, w_in_ref[...], preferred_element_type=F32), approximate=True
        ).astype(BF16)
        result = (values + jnp.dot(hidden, w_out_ref[...], preferred_element_type=F32)).astype(BF16)
        for r4 in range(4):
            res[rg * 4 + r4] = result[r4 * CHUNKP : r4 * CHUNKP + CHUNK]
        for piece in ((0,), (1, 2), (3,))[rg]:
            halo(piece).start()
    own = pltpu.make_async_copy(res, own_ref, own_sem)
    own.start()
    for rg in range(3):

        def finish(k, carry):
            copy(rg, k, 1).wait_send()
            return carry

        lax.fori_loop(1, NCH, finish, 0)
    for piece in range(4):
        halo(piece).wait_send()
        halo(piece).wait_recv()
    own.wait()


def run_tail(state, w_in, w_out):
    return pl.pallas_call(
        tail_kernel,
        in_specs=[pl.BlockSpec(memory_space=pl.ANY)] + [pl.BlockSpec(memory_space=pltpu.VMEM)] * 3,
        out_specs=[pl.BlockSpec(memory_space=pl.ANY)] * 3,
        scratch_shapes=[
            pltpu.VMEM((NCH, CHUNKP, ROWS * CW), BF16),
            pltpu.VMEM((ROWS, CHUNK, 256), BF16),
            pltpu.VMEM((4 * CHUNKP, 256), F32),
            pltpu.SemaphoreType.DMA((3, NCH)),
            pltpu.SemaphoreType.DMA((3, NCH)),
            pltpu.SemaphoreType.DMA((3,)),
            pltpu.SemaphoreType.DMA((4,)),
            pltpu.SemaphoreType.DMA((4,)),
            pltpu.SemaphoreType.DMA,
        ],
        out_shape=[
            jax.ShapeDtypeStruct((ROWS, CHUNK, 256), BF16),
            jax.ShapeDtypeStruct((HALO, CHUNK, 256), BF16),
            jax.ShapeDtypeStruct((HALO, CHUNK, 256), BF16),
        ],
        compiler_params=pltpu.CompilerParams(
            vmem_limit_bytes=VMEM_LIMIT, collective_id=4, has_side_effects=True
        ),
        name="pointwise_tail",
    )(state, w_in, w_out, jnp.asarray(swap_table()))


def assemble_kernel(place_ref, left_ref, own_ref, right_ref, out_ref, scr):
    scr[...] = jnp.zeros_like(scr)
    for at, ref in ((0, left_ref), (HALO, own_ref), (HALO + ROWS, right_ref)):
        for k in range(ref.shape[0]):
            row = at + k + place_ref[0]

            @pl.when((row >= 0) & (row < place_ref[1]))
            def _():
                for h in range(2):
                    scr.at[h][pl.ds(row, CHUNK, stride=24), :] = ref[
                        k, :, h * 128 : h * 128 + 128
                    ].astype(F32)

    for h in range(2):
        out_ref[:, h * 128 : h * 128 + 128] = scr[h].astype(BF16)


def run_assemble(place, pieces):
    return pl.pallas_call(
        assemble_kernel,
        in_specs=[pl.BlockSpec(memory_space=pltpu.SMEM)] + [pl.BlockSpec(memory_space=pltpu.VMEM)] * 3,
        out_specs=pl.BlockSpec(memory_space=pltpu.VMEM),
        scratch_shapes=[pltpu.VMEM((2, CHUNK * 24, 128), F32)],
        out_shape=jax.ShapeDtypeStruct((CHUNK * 24, 256), BF16),
        compiler_params=pltpu.CompilerParams(vmem_limit_bytes=VMEM_LIMIT),
        name="assemble_bands",
    )(place, *pieces)


def partner(kind, index):
    y, z, c = lax.axis_index("y"), lax.axis_index("z"), lax.axis_index("chan")
    if kind == "lat":
        return (index // NZ, index % NZ, c)
    if kind == "own":
        return (index // NCH, z, index % NCH)
    return (y, z, index)


def own_index(kind):
    y, z, c = lax.axis_index("y"), lax.axis_index("z"), lax.axis_index("chan")
    if kind == "lat":
        return y * NZ + z
    if kind == "own":
        return y * NCH + c
    return c


def zigzag(j, n):
    half = (j + 1) // 2
    return jnp.where(j % 2 == 1, half, lax.rem(n - half, n))


def peer_of(kind, k, sign):
    me = own_index(kind)
    if kind == "chan":
        return lax.rem(me + sign * k + NCH, NCH)
    n = NLATD - k
    fast, slow = n // NY, n % NY
    y = lax.rem(me // 8 + sign * zigzag(slow, NY) + NY, NY)
    low = me % 8
    if kind == "lat":
        return y * 8 + lax.rem(low + sign * zigzag(fast, NZ) + NZ, NZ)
    x = lax.rem(low // 2 + sign * zigzag(fast // 2, 4) + 4, 4)
    return y * 8 + x * 2 + lax.rem(low % 2 + fast % 2, 2)


def greet(kind, n, barrier):
    me = own_index(kind)

    def one(k, carry):
        pl.semaphore_signal(
            barrier,
            inc=1,
            device_id=partner(kind, lax.rem(me + k, n)),
            device_id_type=pl.DeviceIdType.MESH,
        )
        return carry

    lax.fori_loop(1, n, one, 0)


def exchange_kernel(kind, n, x_ref, o_ref, send_sem, recv_sem, local_sem):
    me = own_index(kind)
    barrier = pltpu.get_barrier_semaphore()
    greet(kind, n, barrier)
    local = pltpu.make_async_copy(x_ref.at[me], o_ref.at[me], local_sem)
    local.start()
    pl.semaphore_wait(barrier, n - 1)

    def copy(k, sign):
        peer = peer_of(kind, k, sign)
        return pltpu.make_async_remote_copy(
            src_ref=x_ref.at[peer],
            dst_ref=o_ref.at[me if sign == 1 else peer],
            send_sem=send_sem.at[k],
            recv_sem=recv_sem.at[k],
            device_id=partner(kind, peer),
            device_id_type=pl.DeviceIdType.MESH,
        )

    def start(k, carry):
        copy(k, 1).start()
        return carry

    lax.fori_loop(1, n, start, 0)

    def finish(k, carry):
        copy(k, 1).wait_send()
        copy(k, -1).wait_recv()
        return carry

    lax.fori_loop(1, n, finish, 0)
    local.wait()


def outbound_kernel(
    x_ref, first_ref, leg_ref, o_ref, out_ref, turned_ref, send_sem, recv_sem, local_sem
):
    group = pl.program_id(0)
    me = own_index("lat")
    barrier = pltpu.get_barrier_semaphore()
    local = pltpu.make_async_copy(x_ref.at[me], o_ref.at[me], local_sem)

    def copy(k, sign):
        peer = peer_of("lat", k, sign)
        return pltpu.make_async_remote_copy(
            src_ref=x_ref.at[peer],
            dst_ref=o_ref.at[me if sign == 1 else peer],
            send_sem=send_sem.at[k],
            recv_sem=recv_sem.at[k],
            device_id=partner("lat", peer),
            device_id_type=pl.DeviceIdType.MESH,
        )

    @pl.when(group == 0)
    def _():
        greet("lat", NLATD, barrier)
        local.start()
        pl.semaphore_wait(barrier, NLATD - 1)

        def start(k, carry):
            copy(k, 1).start()
            return carry

        lax.fori_loop(1, NLATD, start, 0)

    for ss in range(SG):
        sx, sy = pair_one_hots(jnp.maximum(first_ref[group * SG + ss], 0))
        table = leg_ref[ss]
        x = jnp.dot(sx, table, preferred_element_type=F32)
        y = jnp.dot(sy, table, preferred_element_type=F32)
        out_ref[ss, :ENTRIES] = x.astype(BF16)
        out_ref[ss, ENTRIES:] = y.astype(BF16)
        turned_ref[ss, 0] = jnp.transpose(x).astype(BF16)
        turned_ref[ss, 1] = jnp.transpose(y).astype(BF16)

    @pl.when(group == NSG - 1)
    def _():
        def finish(k, carry):
            copy(k, 1).wait_send()
            copy(k, -1).wait_recv()
            return carry

        lax.fori_loop(1, NLATD, finish, 0)
        local.wait()


def run_outbound(spectra, first, legendre):
    return pl.pallas_call(
        outbound_kernel,
        grid=(NSG,),
        in_specs=[
            pl.BlockSpec(memory_space=pl.ANY),
            pl.BlockSpec(memory_space=pltpu.SMEM),
            pl.BlockSpec((SG, KP, NLATD * ROWS), lambda g: (g, 0, 0)),
        ],
        out_specs=[
            pl.BlockSpec(memory_space=pl.ANY),
            pl.BlockSpec((SG, 2 * ENTRIES, NLATD * ROWS), lambda g: (g, 0, 0)),
            pl.BlockSpec((SG, 2, NLATD * ROWS, ENTRIES), lambda g: (g, 0, 0, 0)),
        ],
        scratch_shapes=[
            pltpu.SemaphoreType.DMA((NLATD,)),
            pltpu.SemaphoreType.DMA((NLATD,)),
            pltpu.SemaphoreType.DMA,
        ],
        out_shape=[
            jax.ShapeDtypeStruct(spectra.shape, BF16),
            jax.ShapeDtypeStruct((SLOTS, 2 * ENTRIES, NLATD * ROWS), BF16),
            jax.ShapeDtypeStruct((SLOTS, 2, NLATD * ROWS, ENTRIES), BF16),
        ],
        compiler_params=pltpu.CompilerParams(
            vmem_limit_bytes=VMEM_LIMIT, collective_id=2, has_side_effects=True
        ),
        name="exchange_out_sort_table",
    )(spectra, first, legendre)


def opening_kernel(
    rows_ref, w_ref, left_ref, right_ref, o_ref, send_sem, recv_sem, local_sem, halo_send, halo_recv
):
    me = own_index("own")
    band = own_index("lat")
    rightward = lax.rem(band + 1, NLATD)
    leftward = lax.rem(band + NLATD - 1, NLATD)
    barrier = pltpu.get_barrier_semaphore()
    for neighbour in (leftward, rightward):
        pl.semaphore_signal(
            barrier, inc=1, device_id=partner("lat", neighbour), device_id_type=pl.DeviceIdType.MESH
        )
    greet("own", 32, barrier)
    local = pltpu.make_async_copy(w_ref.at[me], o_ref.at[me], local_sem)
    local.start()
    pl.semaphore_wait(barrier, 33)

    def halo(side):
        return pltpu.make_async_remote_copy(
            src_ref=rows_ref.at[pl.ds(side * (HALO + ROWS), HALO)],
            dst_ref=left_ref if side else right_ref,
            send_sem=halo_send.at[side],
            recv_sem=halo_recv.at[side],
            device_id=partner("lat", rightward if side else leftward),
            device_id_type=pl.DeviceIdType.MESH,
        )

    def copy(k, sign):
        peer = peer_of("own", k, sign)
        return pltpu.make_async_remote_copy(
            src_ref=w_ref.at[peer],
            dst_ref=o_ref.at[me if sign == 1 else peer],
            send_sem=send_sem.at[k],
            recv_sem=recv_sem.at[k],
            device_id=partner("own", peer),
            device_id_type=pl.DeviceIdType.MESH,
        )

    for side in range(2):
        halo(side).start()

    def start(k, carry):
        copy(k, 1).start()
        return carry

    lax.fori_loop(1, 32, start, 0)

    def finish(k, carry):
        copy(k, 1).wait_send()
        copy(k, -1).wait_recv()
        return carry

    lax.fori_loop(1, 32, finish, 0)
    local.wait()
    for side in range(2):
        halo(side).wait_send()
        halo(side).wait_recv()


def run_opening(rows, by_degree):
    return pl.pallas_call(
        opening_kernel,
        in_specs=[pl.BlockSpec(memory_space=pl.ANY)] * 2,
        out_specs=[pl.BlockSpec(memory_space=pl.ANY)] * 3,
        scratch_shapes=[
            pltpu.SemaphoreType.DMA((32,)),
            pltpu.SemaphoreType.DMA((32,)),
            pltpu.SemaphoreType.DMA,
            pltpu.SemaphoreType.DMA((2,)),
            pltpu.SemaphoreType.DMA((2,)),
        ],
        out_shape=[
            jax.ShapeDtypeStruct((HALO, CW, NLON), BF16),
            jax.ShapeDtypeStruct((HALO, CW, NLON), BF16),
            jax.ShapeDtypeStruct(by_degree.shape, BF16),
        ],
        compiler_params=pltpu.CompilerParams(collective_id=0, has_side_effects=True),
        name="opening_exchange",
    )(rows, by_degree)


def exchange(kind, collective, x):
    n = x.shape[0]
    return pl.pallas_call(
        functools.partial(exchange_kernel, kind, n),
        in_specs=[pl.BlockSpec(memory_space=pl.ANY)],
        out_specs=pl.BlockSpec(memory_space=pl.ANY),
        scratch_shapes=[
            pltpu.SemaphoreType.DMA((n,)),
            pltpu.SemaphoreType.DMA((n,)),
            pltpu.SemaphoreType.DMA,
        ],
        out_shape=jax.ShapeDtypeStruct(x.shape, x.dtype),
        compiler_params=pltpu.CompilerParams(collective_id=collective, has_side_effects=True),
        name="exchange_" + kind,
    )(x)


def order_columns(pairing):
    a = pairing.reshape(NLATD, 1, SLOTS)
    return jnp.where(a >= 0, jnp.concatenate([a, L - 1 - a], axis=1), -1)


def one_hot(col, width):
    return (col.reshape(-1)[:, None] == jnp.arange(width, dtype=jnp.int32)[None, :]).astype(BF16)


def dot_nt(a, b):
    return lax.dot_general(a, b, (((1,), (1,)), ((), ())), preferred_element_type=F32)


def per_device(grid_in, pairing, offsets, legendre, degree_mix, w_in, w_out):
    lat = ("y", "z")
    me = lax.axis_index("y") * NZ + lax.axis_index("z")
    chan = lax.axis_index("chan")
    start = jnp.take(offsets, me)
    length = jnp.take(offsets, me + 1) - start
    first = lax.dynamic_slice_in_dim(pairing, me * SLOTS, SLOTS)
    cap = grid_in.shape[0]

    rows = jnp.transpose(grid_in, (0, 2, 1))
    valid = (jnp.arange(cap, dtype=jnp.int32) < length)[:, None, None]
    rows = jnp.where(valid, rows, jnp.zeros((), BF16))
    shift = me * ROWS - HALO - start
    rows = jnp.concatenate([jnp.zeros((12, CW, NLON), BF16), rows], axis=0)
    virt = lax.dynamic_slice_in_dim(rows, 12 + shift, cap, axis=0)
    own = virt[HALO : HALO + ROWS]
    by_degree = dot_nt(
        jnp.asarray(degree_order()),
        jnp.transpose(degree_mix, (1, 2, 0)).reshape(8 * CW, L),
    ).astype(BF16)
    from_left, from_right, owned = run_opening(virt, by_degree.reshape(32, 2 * JO, 256))
    xt = (own + jnp.concatenate([from_left, from_right], axis=0)).reshape(ROWS * CW, NLON)
    gathered = lax.all_gather(owned, "z", axis=0, tiled=False)
    weights = run_weights(gathered)
    weights = weights.reshape(2 * JO, 256, 256)

    sides = order_columns(pairing)
    home = one_hot(sides.reshape(NLATD, 2, NSG, SG).transpose(2, 0, 1, 3), L)
    waves_back = inverse_table()
    inverse_re = dot_nt(jnp.asarray(waves_back[:, :L]), home).astype(BF16)
    inverse_im = dot_nt(jnp.asarray(waves_back[:, L:]), home).astype(BF16)
    padded = dot_nt(jnp.asarray(pad_rows()), xt).astype(BF16)

    waves = forward_table()
    by_order = lax.optimization_barrier(
        jnp.concatenate(
            [dot_nt(jnp.asarray(waves[:L]), xt).astype(BF16), dot_nt(jnp.asarray(waves[L:]), xt).astype(BF16)],
            axis=1,
        )
    )
    spectra = jnp.dot(one_hot(sides, L), by_order, preferred_element_type=F32).astype(BF16)
    incoming, table, turned = run_outbound(
        spectra.reshape(NLATD, 24, 2 * ROWS * CW), first, legendre
    )
    coeffs = run_legendre(first, incoming.reshape(NLATD * 24, 2 * ROWS * CW), table)
    at_owner = lax.all_to_all(
        coeffs.reshape(32, MROWS, 128), ("y", "chan"), split_axis=0, concat_axis=0, tiled=True
    )
    at_owner, weights, inverse_re, inverse_im, padded = lax.optimization_barrier(
        (at_owner, weights, inverse_re, inverse_im, padded)
    )
    owner = (lax.axis_index("y") * NCH + chan).reshape(1)
    z = lax.axis_index("z")
    a_here = lax.dynamic_slice_in_dim(pairing.reshape(NY, NZ, SLOTS), z, 1, axis=1)[:, 0]
    a_here = jnp.concatenate([a_here, jnp.full((NY, 4), -1, jnp.int32)], axis=1).reshape(1, NY * 16)
    a_here = jnp.broadcast_to(a_here, (2, NY * 16)).reshape(128, 1)
    mixed = run_mix(owner, at_owner, weights, a_here)
    returned = exchange("own", 1, mixed)
    spectrum, homeward = run_inverse(first, returned.reshape(32 * MROWS, 128), turned)
    spectrum = jnp.transpose(spectrum.reshape(SLOTS, 2, CW, KP), (0, 3, 1, 2))
    homeward = homeward.reshape(NLATD * 24, 2 * ROWS * CW)
    filtered = jnp.dot(
        inverse_re, homeward[:, : ROWS * CW], preferred_element_type=F32
    ) + jnp.dot(inverse_im, homeward[:, ROWS * CW :], preferred_element_type=F32)
    state = (padded.astype(F32) + filtered).astype(BF16)
    own_rows, out_left, out_right = run_tail(state.reshape(NCH, CHUNKP, ROWS * CW), w_in, w_out)
    place = jnp.stack([shift, length])
    grid_out = run_assemble(place, (out_left, own_rows, out_right))
    grid_out = jnp.transpose(grid_out.reshape(CHUNK, cap, 256), (1, 0, 2))
    return (grid_out, spectrum)


def solution(mesh):
    fine = Mesh(np.asarray(mesh.devices).reshape(NY, NZ, NCH), ("y", "z", "chan"))
    lat = ("y", "z")
    in_specs = (
        P(lat, None, "chan"),
        P(),
        P(),
        P(lat, None, None),
        P(None, lat, "chan"),
        P(),
        P(),
    )
    out_specs = (P(lat, "chan", None), P(lat, None, None, "chan"))
    return jax.shard_map(per_device, mesh=fine, in_specs=in_specs, out_specs=out_specs, check_vma=False)
```

profile of v0, /device:TPU:1, one launch (start us, length us, event | category | flops | bytes accessed | tf_op | source)
XLA Modules:
  0.0 261.1 jit_solution(14099758869314011044)
XLA Ops:
  7.2 1.4 fusion.17
  10.0 1.9 select_bitcast_fusion
  11.9 1.8 pad_dynamic-slice_fusion.1.rows_ref
  13.7 1.3 convolution_convert_fusion.5
  15.0 29.1 %opening_exchange.1 = (bf16[6,32,1440]{2,1,0:T(8,128)(2,1)}, bf16[6,32,1440]{2,1,0:T(8,128)(2,1)}, bf16[32,24,256]{2,1,0:T(8,128)(2,1)}) custom-call(bf16[24,32,1440]{2,1,0:T(8,128)(2,1)} %pad_dynamic-slice_fusion.1.rows_ref, bf16[32,24,256]{2,1,0:T(8,128)(2,1)} %bitcast.60), custom_call_target="tpu_custom_call" | custom-call | tf_op jit(solution)/shard_map/opening_exchange/pallas_call | solution.py:824
  44.2 0.1 reshape.111
  44.3 0.6 dynamic_slice.9.first_ref
  44.9 1.7 fusion.9
  46.6 0.3 copy-done.11
  46.9 1.3 fusion.8
  48.2 0.4 copy-done.10
  48.6 1.3 fusion.7
  50.0 0.1 pad_maximum_fusion
  50.1 0.1 copy.31
  50.2 0.1 copy.32
  50.2 0.1 ge.29
  50.4 0.1 copy.30
  50.5 0.1 copy.33
  50.6 0.1 select_n.51
  50.7 2.2 fusion.6
  52.9 48.2 %exchange_out_sort_table.1 = (bf16[32,24,768]{2,1,0:T(8,128)(2,1)}, bf16[12,832,384]{2,1,0:T(8,128)(2,1)}, bf16[12,2,384,416]{3,2,1,0:T(8,128)(2,1)}) custom-call(bf16[32,24,768]{2,1,0:T(8,128)(2,1)} %bitcast.61, s32[12]{0:T(128)} %dynamic_slice.9.first_ref, bf16[12,721,384]{2,1,0:T(8,128)(2,1)} %leg_ref.1), custom_call_target="tpu_custom_call" | custom-call | tf_op jit(solution)/shard_map/exchange_out_sort_table/pallas_call | solution.py:734
  101.1 12.1 %legendre_forward.1 = bf16[5120,128]{1,0:T(8,128)(2,1)} custom-call(s32[12]{0:T(128)} %dynamic_slice.9.first_ref, bf16[768,768]{1,0:T(8,128)(2,1)} %bitcast.66, bf16[12,832,384]{2,1,0:T(8,128)(2,1)} %get-tuple-element.21.leg_ref, bf16[512,1024]{1,0:T(8,128)(2,1)} %constant.84.clone.swap_ref), custom_call_target="tpu_custom_call" | custom-call | tf_op jit(solution)/shard_map/legendre_forward/pallas_call | solution.py:161
  113.2 7.1 %all-to-all-start = ((bf16[32,160,128]{2,1,0:T(8,128)(2,1)}), bf16[32,160,128]{2,1,0:T(8,128)(2,1)S(1)}, u32[]{:S(2)}, u32[]{:S(2)}) async-start(bf16[32,160,128]{2,1,0:T(8,128)(2,1)} %bitcast.55), calls=%async_computation | async-start | bytes 2621440 | tf_op jit(solution)/shard_map/all_to_all | solution.py:920
  120.3 0.1 concatenate.24
  120.4 0.1 ge.30
  120.6 0.1 reshape.120
  120.7 0.1 copy.35
  120.8 0.1 copy.36
  120.9 0.1 copy.34
  121.0 0.1 copy.37
  121.1 0.2 eq.31
  121.3 0.1 broadcast_in_dim.54
  121.4 0.8 reshape.186.a_ref
  122.2 0.7 pad_add_fusion.place_ref
  122.9 5.3 %fusion = bf16[1536,768]{0,1:T(8,128)(2,1)} fusion(bf16[1536,720]{1,0:T(8,128)(2,1)} %constant.79.clone, s32[768]{0:T(1024)S(1)} %eq.31), kind=kOutput, calls=%fused_computation.5 | convolution fusion | flops 1700425728 | bytes 4574208 | tf_op jit(solution)/shard_map/dot_general | solution.py:872
  128.1 3.4 %fusion.1 = bf16[1536,768]{0,1:T(8,128)(2,1)} fusion(bf16[1536,720]{1,0:T(8,128)(2,1)S(1)} %copy-done.9, s32[768]{0:T(1024)S(1)} %eq.31), kind=kOutput, calls=%fused_computation.6 | convolution fusion | flops 1700425728 | bytes 4574208 | tf_op jit(solution)/shard_map/dot_general | solution.py:872
  131.6 2.1 fusion.4
  133.7 8.2 %unpack_weights.1 = bf16[24,4,8,8,256]{4,3,2,1,0:T(8,128)(2,1)} custom-call(bf16[8,32,24,256]{3,2,1,0:T(8,128)(2,1)} %bitcast.68, bf16[512,512]{1,0:T(8,128)(2,1)} %constant.78.clone.swap_ref), custom_call_target="tpu_custom_call" | custom-call | flops 4000000000 | bytes 6000000 | tf_op jit(solution)/shard_map/unpack_weights/pallas_call | solution.py:212
  141.9 1.1 copy-done.2
  143.0 6.2 %mix_degrees.1.x_ref = bf16[32,160,128]{2,1,0:T(8,128)(2,1)} custom-call(s32[1]{0:T(128)} %bitcast.22.owner_ref, bf16[32,160,128]{2,1,0:T(8,128)(2,1)} %copy-done.2, bf16[24,256,256]{2,1,0:T(8,128)(2,1)} %bitcast.58, s32[128,1]{1,0:T(8,128)} %reshape.186.a_ref, bf16[512,512]{1,0:T(8,128)(2,1)} %constant.78.clone.swap_ref), custom_call_target="tpu_custom_call" | custom-call | tf_op jit(solution)/shard_map/mix_degrees/pallas_call | solution.py:290
  149.2 22.8 %exchange_own.1 = bf16[32,160,128]{2,1,0:T(8,128)(2,1)} custom-call(bf16[32,160,128]{2,1,0:T(8,128)(2,1)} %mix_degrees.1.x_ref), custom_call_target="tpu_custom_call" | custom-call | tf_op jit(solution)/shard_map/exchange_own/pallas_call | solution.py:847
  172.0 39.1 %legendre_inverse_home.1 = (bf16[12,64,721]{2,1,0:T(8,128)(2,1)}, bf16[3,32,8,768]{3,2,1,0:T(8,128)(2,1)}) custom-call(s32[12]{0:T(128)} %dynamic_slice.9.first_ref, bf16[5120,128]{1,0:T(8,128)(2,1)} %bitcast.56, bf16[12,2,384,416]{3,2,1,0:T(8,128)(2,1)} %get-tuple-element.27.turned_ref, bf16[512,512]{1,0:T(8,128)(2,1)} %constant.78.clone.swap_ref), custom_call_target="tpu_custom_call" | custom-call | tf_op jit(solution)/shard_map/legendre_inverse_home/pallas_call | solution.py:406
  211.2 2.3 fusion.14
  213.5 1.2 fusion.3
  214.7 1.4 copy.41
  216.1 32.8 %pointwise_tail.1 = (bf16[12,180,256]{2,1,0:T(8,128)(2,1)}, bf16[6,180,256]{2,1,0:T(8,128)(2,1)}, bf16[6,180,256]{2,1,0:T(8,128)(2,1)}) custom-call(bf16[8,192,384]{2,1,0:T(8,128)(2,1)} %bitcast.57, bf16[256,512]{1,0:T(8,128)(2,1)} %w_in_ref.1, bf16[512,256]{1,0:T(8,128)(2,1)} %w_out_ref.1, bf16[512,512]{1,0:T(8,128)(2,1)} %constant.78.clone.swap_ref), custom_call_target="tpu_custom_call" | custom-call | tf_op jit(solution)/shard_map/pointwise_tail/pallas_call | solution.py:539
  249.0 4.2 %assemble_bands.1 = bf16[4320,256]{1,0:T(8,128)(2,1)} custom-call(s32[2]{0:T(128)} %pad_add_fusion.place_ref, bf16[6,180,256]{2,1,0:T(8,128)(2,1)} %get-tuple-element.30.left_ref, bf16[12,180,256]{2,1,0:T(8,128)(2,1)} %get-tuple-element.31.own_ref, bf16[6,180,256]{2,1,0:T(8,128)(2,1)} %get-tuple-element.32.right_ref), custom_call_target="tpu_custom_call" | custom-call | tf_op jit(solution)/shard_map/assemble_bands/pallas_call | solution.py:584
  253.2 1.0 copy.45
  (43 shorter events, 0.3 us)
Async XLA Ops:
  7.2 6.6 %copy-start = (bf16[720,8,32]{0,2,1:T(8,128)(2,1)S(1)}, bf16[720,8,32]{0,2,1:T(8,128)(2,1)}, u32[]{:S(2)}) copy-start(bf16[720,8,32]{0,2,1:T(8,128)(2,1)} %param.22) | copy-start | bytes 1105924
  7.2 126.5 %all-gather.3.cloned.1.call-start = ((), (), s32[]{:S(2)}) async-start(), calls=%async_computation.1 | async-start | bytes 3538944 | tf_op jit(solution)/shard_map/all_gather | solution.py:897
  11.9 1.8 copy-start.6
  13.7 30.4 %copy-start.7 = (s32[384]{0:T(512)S(1)}, s32[384]{0:T(512)}, u32[]{:S(2)}) copy-start(s32[384]{0:T(512)} %param.19) | copy-start | bytes 4612
  44.9 2.0 copy-start.11
  46.6 1.6 copy-start.3
  46.9 1.8 copy-start.10
  113.2 28.7 %all-to-all-start = ((bf16[32,160,128]{2,1,0:T(8,128)(2,1)}), bf16[32,160,128]{2,1,0:T(8,128)(2,1)S(1)}, u32[]{:S(2)}, u32[]{:S(2)}) async-start(bf16[32,160,128]{2,1,0:T(8,128)(2,1)} %bitcast.55), calls=%async_computation | async-start | bytes 2621440 | tf_op jit(solution)/shard_map/all_to_all | solution.py:920
  122.9 5.3 %copy-start.9 = (bf16[1536,720]{1,0:T(8,128)(2,1)S(1)}, bf16[1536,720]{1,0:T(8,128)(2,1)}, u32[]{:S(2)}) copy-start(bf16[1536,720]{1,0:T(8,128)(2,1)} %constant.80.clone) | copy-start | bytes 6635524
  122.9 8.7 %slice-start = ((s8[4718592]{0:T(1024)(128)(4,1)}), s8[4194304]{0:T(1024)(128)(4,1)S(1)}, s32[]{:S(2)}) async-start(s8[4718592]{0:T(1024)(128)(4,1)} %bitcast.71), calls=%async_computation.2 | async-start | bytes 8388608
  128.1 3.4 %copy-start.4 = (bf16[12,32,1440]{2,1,0:T(8,128)(2,1)S(1)}, bf16[12,32,1440]{2,1,0:T(8,128)(2,1)}, u32[]{:S(2)}) copy-start(bf16[12,32,1440]{2,1,0:T(8,128)(2,1)} %copy-done.3) | copy-start | bytes 3317764
  128.1 3.4 %slice-start.1 = ((s8[4718592]{0:T(1024)(128)(4,1)}), s8[524288]{0:T(1024)(128)(4,1)S(1)}, s32[]{:S(2)}) async-start(s8[4718592]{0:T(1024)(128)(4,1)} %bitcast.71), calls=%async_computation.3 | async-start | bytes 1048576
  141.9 1.1 copy-start.2
  172.0 39.1 %copy-start.12 = (bf16[1536,768]{0,1:T(8,128)(2,1)S(1)}, bf16[1536,768]{0,1:T(8,128)(2,1)}, u32[]{:S(2)}) copy-start(bf16[1536,768]{0,1:T(8,128)(2,1)} %fusion) | copy-start | bytes 7077892
  211.1 2.4 copy-start.8
  211.1 2.4 copy-start.13
  249.0 4.3 %copy-start.5 = (bf16[12,64,721]{2,1,0:T(8,128)(2,1)S(1)}, bf16[12,64,721]{2,1,0:T(8,128)(2,1)}, u32[]{:S(2)}) copy-start(bf16[12,64,721]{2,1,0:T(8,128)(2,1)} %get-tuple-element.33) | copy-start | bytes 3322372
  249.0 5.3 %copy-start.1 = (bf16[720,8,32]{0,2,1:T(8,128)(2,1)S(1)}, bf16[720,8,32]{0,2,1:T(8,128)(2,1)}, u32[]{:S(2)}) copy-start(bf16[720,8,32]{0,2,1:T(8,128)(2,1)} %param.22) | copy-start | bytes 1105924
Sparse Core Ops, SparseCore 0:
  44.3 66.6 all-gather.2
where the time goes:
time: 262 us; the launch traced here: 261 us
  Pallas kernels  203 us (77%)
  matrix products  20.4 us (8%)
  between operations  15.7 us (6%)
  local copies, waits for them, and re-layouts  10.5 us (4%)
  starting transfers between devices  7.13 us (3%)
  other arithmetic  4.42 us (2%)
    pallas_call x1, Pallas kernels, run_outbound(): pl.pallas_call(outbound_kernel, grid=(NSG,), in_specs=[pl.BlockSpec(memor...  48.2 us
    pallas_call x1, Pallas kernels, run_inverse(): pl.pallas_call(inverse_kernel, grid=(NSG,), in_specs=[pl.BlockSpec(memory...  39.1 us
    pallas_call x1, Pallas kernels, run_tail(): pl.pallas_call(tail_kernel, in_specs=[pl.BlockSpec(memory_space=pl.ANY)]...  32.8 us
    pallas_call x1, Pallas kernels, run_opening(): pl.pallas_call(opening_kernel, in_specs=[pl.BlockSpec(memory_space=pl.ANY...  29.1 us
    pallas_call x1, Pallas kernels, exchange(): pl.pallas_call(functools.partial(exchange_kernel, kind, n), in_specs=[pl....  22.8 us
    dot_general x6, matrix products, dot_nt(): lax.dot_general(a, b, (((1,), (1,)), ((), ())), preferred_element_type=F32)  14.7 us
    pallas_call x1, Pallas kernels, run_legendre(): pl.pallas_call(legendre_kernel, grid_spec=pltpu.PrefetchScalarGridSpec(nu...  12.1 us
    pallas_call x1, Pallas kernels, run_weights(): pl.pallas_call(weights_kernel, grid=(NZ // 2,), in_specs=[pl.BlockSpec((2...  8.22 us
  transfers between devices with their start and end apart: 2, of which 0 were waited for; matrix products, arithmetic and copies ran while one was open for 8% of the time, Pallas kernels for 26%

commit v1 on v0

--- a/solution.py
+++ b/solution.py
@@ -112,73 +112,30 @@
     return sx, sy
 
 
-def legendre_kernel(first_ref, inc_ref, leg_ref, swap_ref, out_ref, scr_f, scr_r, scr_o):
-    group = pl.program_id(0)
-
-    @pl.when(group == 0)
-    def _():
-        for k in range(6):
-            scr_f[k] = inc_ref[:, k * 128 : k * 128 + 128].astype(F32)
-        scr_o[...] = jnp.zeros_like(scr_o)
-
+def legendre_slot(s, part, base, scr_f, table, swap, scr_r, scr_o):
     row = lax.broadcasted_iota(jnp.int32, (ENTRIES, 128), 0)
     lane = lax.broadcasted_iota(jnp.int32, (ENTRIES, 128), 1)
     degree = JO * (row % 32) + row // 32
-    for ss in range(SG):
-        s = group * SG + ss
-        t = [
-            jnp.concatenate(
-                [
-                    scr_f.at[p * 3 + rg][pl.ds(side * SLOTS + s, 32, stride=24), :]
-                    for rg in range(3)
-                ],
-                axis=0,
-            )
-            for side in range(2)
-            for p in range(2)
-        ]
-        for r4, u in enumerate(swap4(t, swap_ref[...])):
-            for rg in range(3):
-                for k in range(2):
-                    scr_r.at[ss * 2 + k][pl.ds(rg * 4 + r4, 32, stride=ROWS), :] = u[
-                        rg * 32 : rg * 32 + 32, k * 128 : k * 128 + 128
-                    ]
-        right = jnp.concatenate([scr_r[ss * 2], scr_r[ss * 2 + 1]], axis=1).astype(BF16)
-        both = jnp.dot(leg_ref[ss], right, preferred_element_type=F32)
-        base = jnp.maximum(first_ref[s], 0)
-        x = jnp.where(row < 32 * JO, both[:ENTRIES, :128], both[:ENTRIES, 128:])
-        y = jnp.where(degree >= base, both[ENTRIES:, 128:], both[ENTRIES:, :128])
-        q = jnp.where(lane < 64, x, y)
-        for jj in range(JR):
-            scr_o[pl.ds(s * JR + jj, 32, stride=MROWS), :] = q[jj * 32 : jj * 32 + 32]
-
-    @pl.when(group == NSG - 1)
-    def _():
-        out_ref[...] = scr_o[...].astype(BF16)
-
-
-def run_legendre(first, incoming, table):
-    return pl.pallas_call(
-        legendre_kernel,
-        grid_spec=pltpu.PrefetchScalarGridSpec(
-            num_scalar_prefetch=1,
-            grid=(NSG,),
-            in_specs=[
-                pl.BlockSpec((NLATD * 24, 2 * ROWS * CW), lambda g, f: (0, 0)),
-                pl.BlockSpec((SG, 2 * ENTRIES, NLATD * ROWS), lambda g, f: (g, 0, 0)),
-                pl.BlockSpec((512, 1024), lambda g, f: (0, 0)),
-            ],
-            out_specs=pl.BlockSpec((32 * MROWS, 128), lambda g, f: (0, 0)),
-            scratch_shapes=[
-                pltpu.VMEM((6, NLATD * 24, 128), F32),
-                pltpu.VMEM((2 * SG, NLATD * ROWS, 128), F32),
-                pltpu.VMEM((32 * MROWS, 128), F32),
-            ],
-        ),
-        out_shape=jax.ShapeDtypeStruct((32 * MROWS, 128), BF16),
-        compiler_params=pltpu.CompilerParams(vmem_limit_bytes=VMEM_LIMIT),
-        name="legendre_forward",
-    )(first, incoming, table, jnp.asarray(swap_mirror_table()))
+    t = [
+        jnp.concatenate(
+            [scr_f.at[p * 3 + rg][pl.ds(side * SLOTS + s, 32, stride=24), :] for rg in range(3)], axis=0
+        )
+        for side in range(2)
+        for p in range(2)
+    ]
+    for r4, u in enumerate(swap4(t, swap)):
+        for rg in range(3):
+            for k in range(2):
+                scr_r.at[part * 2 + k][pl.ds(rg * 4 + r4, 32, stride=ROWS), :] = u[
+                    rg * 32 : rg * 32 + 32, k * 128 : k * 128 + 128
+                ]
+    right = jnp.concatenate([scr_r[part * 2], scr_r[part * 2 + 1]], axis=1).astype(BF16)
+    both = jnp.dot(table[s], right, preferred_element_type=F32)
+    x = jnp.where(row < 32 * JO, both[:ENTRIES, :128], both[:ENTRIES, 128:])
+    y = jnp.where(degree >= base, both[ENTRIES:, 128:], both[ENTRIES:, :128])
+    q = jnp.where(lane < 64, x, y)
+    for jj in range(JR):
+        scr_o[pl.ds(s * JR + jj, 32, stride=MROWS), :] = q[jj * 32 : jj * 32 + 32]
 
 
 def weights_kernel(w_ref, swap_ref, out_ref, scr):
@@ -228,7 +185,12 @@
 VROWS = NY * MROWS
 
 
-def mix_kernel(owner_ref, d_ref, w_ref, a_ref, swap_ref, out_ref, v, ex):
+def mix_kernel(
+    owner_ref, d_ref, w_ref, a_ref, swap_ref, home_ref, v, ex, leaving, send_sem, recv_sem, local_sem
+):
+    me = own_index("own")
+    barrier = pltpu.get_barrier_semaphore()
+    greet("own", 32, barrier)
     for y in range(NY):
         for h in range(2):
             t = [d_ref[y * 8 + h * 4 + i] for i in range(4)]
@@ -283,7 +245,35 @@
                 for q in range(4)
             ]
             for i, u in enumerate(swap4(t, swap_ref[...])):
-                out_ref[y * 8 + h * 4 + i] = u.astype(BF16)
+                leaving[y * 8 + h * 4 + i] = u.astype(BF16)
+    local = pltpu.make_async_copy(leaving.at[me], home_ref.at[me], local_sem)
+    local.start()
+    pl.semaphore_wait(barrier, 31)
+
+    def copy(k, sign):
+        peer = peer_of("own", k, sign)
+        return pltpu.make_async_remote_copy(
+            src_ref=leaving.at[peer],
+            dst_ref=home_ref.at[me if sign == 1 else peer],
+            send_sem=send_sem.at[k],
+            recv_sem=recv_sem.at[k],
+            device_id=partner("own", peer),
+            device_id_type=pl.DeviceIdType.MESH,
+        )
+
+    def start(k, carry):
+        copy(k, 1).start()
+        return carry
+
+    lax.fori_loop(1, 32, start, 0)
+
+    def finish(k, carry):
+        copy(k, 1).wait_send()
+        copy(k, -1).wait_recv()
+        return carry
+
+    lax.fori_loop(1, 32, finish, 0)
+    local.wait()
 
 
 def run_mix(owner, coeffs, weights, lower_orders):
@@ -296,10 +286,17 @@
             pl.BlockSpec(memory_space=pltpu.VMEM),
             pl.BlockSpec(memory_space=pltpu.VMEM),
         ],
-        out_specs=pl.BlockSpec(memory_space=pltpu.VMEM),
-        scratch_shapes=[pltpu.VMEM((2, 4 * VROWS + 64, 128), F32), pltpu.VMEM((128, 256), F32)],
+        out_specs=pl.BlockSpec(memory_space=pl.ANY),
+        scratch_shapes=[pltpu.VMEM((2, 4 * VROWS + 64, 128), F32), pltpu.VMEM((128, 256), F32),
+            pltpu.VMEM((32, MROWS, 128), BF16),
+            pltpu.SemaphoreType.DMA((32,)),
+            pltpu.SemaphoreType.DMA((32,)),
+            pltpu.SemaphoreType.DMA,
+        ],
         out_shape=jax.ShapeDtypeStruct((32, MROWS, 128), BF16),
-        compiler_params=pltpu.CompilerParams(vmem_limit_bytes=VMEM_LIMIT),
+        compiler_params=pltpu.CompilerParams(
+            vmem_limit_bytes=VMEM_LIMIT, collective_id=1, has_side_effects=True
+        ),
         name="mix_degrees",
     )(owner, coeffs, weights, lower_orders, jnp.asarray(swap_table()))
 
@@ -437,6 +434,7 @@
     )(first, mixed, turned, jnp.asarray(swap_table()))
 
 
+GROUP_ORDER = (0, 2, 1)
 PIECES = ((0, 4, 0), (4, 6, 4), (6, 8, 0), (8, 12, 2))
 
 
@@ -475,13 +473,21 @@
             device_id_type=pl.DeviceIdType.MESH,
         )
 
-    for rg in range(3):
-
+    def start_group(rg):
         def start(k, carry):
             copy(rg, k, 1).start()
             return carry
 
         lax.fori_loop(1, NCH, start, 0)
+
+    def group_left(rg):
+        def finish(k, carry):
+            copy(rg, k, 1).wait_send()
+            return carry
+
+        lax.fori_loop(1, NCH, finish, 0)
+
+    start_group(GROUP_ORDER[0])
 
     def halo(piece):
         first, last, place = PIECES[piece]
@@ -495,7 +501,10 @@
             device_id_type=pl.DeviceIdType.MESH,
         )
 
-    for rg in range(3):
+    for place, rg in enumerate(GROUP_ORDER):
+        group_left(rg)
+        if place < 2:
+            start_group(GROUP_ORDER[place + 1])
 
         def arrive(k, carry):
             copy(rg, k, -1).wait_recv()
@@ -522,13 +531,6 @@
             halo(piece).start()
     own = pltpu.make_async_copy(res, own_ref, own_sem)
     own.start()
-    for rg in range(3):
-
-        def finish(k, carry):
-            copy(rg, k, 1).wait_send()
-            return carry
-
-        lax.fori_loop(1, NCH, finish, 0)
     for piece in range(4):
         halo(piece).wait_send()
         halo(piece).wait_recv()
@@ -644,53 +646,20 @@
     lax.fori_loop(1, n, one, 0)
 
 
-def exchange_kernel(kind, n, x_ref, o_ref, send_sem, recv_sem, local_sem):
-    me = own_index(kind)
-    barrier = pltpu.get_barrier_semaphore()
-    greet(kind, n, barrier)
-    local = pltpu.make_async_copy(x_ref.at[me], o_ref.at[me], local_sem)
-    local.start()
-    pl.semaphore_wait(barrier, n - 1)
-
-    def copy(k, sign):
-        peer = peer_of(kind, k, sign)
-        return pltpu.make_async_remote_copy(
-            src_ref=x_ref.at[peer],
-            dst_ref=o_ref.at[me if sign == 1 else peer],
-            send_sem=send_sem.at[k],
-            recv_sem=recv_sem.at[k],
-            device_id=partner(kind, peer),
-            device_id_type=pl.DeviceIdType.MESH,
-        )
-
-    def start(k, carry):
-        copy(k, 1).start()
-        return carry
-
-    lax.fori_loop(1, n, start, 0)
-
-    def finish(k, carry):
-        copy(k, 1).wait_send()
-        copy(k, -1).wait_recv()
-        return carry
-
-    lax.fori_loop(1, n, finish, 0)
-    local.wait()
-
-
 def outbound_kernel(
-    x_ref, first_ref, leg_ref, o_ref, out_ref, turned_ref, send_sem, recv_sem, local_sem
+    x_ref, first_ref, leg_ref, swap_ref, coeff_ref, turned_ref,
+    arrived, table, scr_f, scr_r, scr_o, send_sem, recv_sem, local_sem,
 ):
     group = pl.program_id(0)
     me = own_index("lat")
     barrier = pltpu.get_barrier_semaphore()
-    local = pltpu.make_async_copy(x_ref.at[me], o_ref.at[me], local_sem)
+    local = pltpu.make_async_copy(x_ref.at[me], arrived.at[me], local_sem)
 
     def copy(k, sign):
         peer = peer_of("lat", k, sign)
         return pltpu.make_async_remote_copy(
             src_ref=x_ref.at[peer],
-            dst_ref=o_ref.at[me if sign == 1 else peer],
+            dst_ref=arrived.at[me if sign == 1 else peer],
             send_sem=send_sem.at[k],
             recv_sem=recv_sem.at[k],
             device_id=partner("lat", peer),
@@ -711,11 +680,11 @@
 
     for ss in range(SG):
         sx, sy = pair_one_hots(jnp.maximum(first_ref[group * SG + ss], 0))
-        table = leg_ref[ss]
-        x = jnp.dot(sx, table, preferred_element_type=F32)
-        y = jnp.dot(sy, table, preferred_element_type=F32)
-        out_ref[ss, :ENTRIES] = x.astype(BF16)
-        out_ref[ss, ENTRIES:] = y.astype(BF16)
+        packed = leg_ref[ss]
+        x = jnp.dot(sx, packed, preferred_element_type=F32)
+        y = jnp.dot(sy, packed, preferred_element_type=F32)
+        table[group * SG + ss, :ENTRIES] = x.astype(BF16)
+        table[group * SG + ss, ENTRIES:] = y.astype(BF16)
         turned_ref[ss, 0] = jnp.transpose(x).astype(BF16)
         turned_ref[ss, 1] = jnp.transpose(y).astype(BF16)
 
@@ -728,6 +697,21 @@
 
         lax.fori_loop(1, NLATD, finish, 0)
         local.wait()
+        for k in range(6):
+            scr_f[k] = (
+                arrived[:, :, k * 128 : k * 128 + 128].astype(F32).reshape(NLATD * 2 * SLOTS, 128)
+            )
+        scr_o[...] = jnp.zeros_like(scr_o)
+
+        def four(g, carry):
+            for ss in range(SG):
+                s = g * SG + ss
+                base = jnp.maximum(first_ref[s], 0)
+                legendre_slot(s, ss, base, scr_f, table, swap_ref[...], scr_r, scr_o)
+            return carry
+
+        lax.fori_loop(0, NSG, four, 0)
+        coeff_ref[...] = scr_o[...].astype(BF16)
 
 
 def run_outbound(spectra, first, legendre):
@@ -738,27 +722,31 @@
             pl.BlockSpec(memory_space=pl.ANY),
             pl.BlockSpec(memory_space=pltpu.SMEM),
             pl.BlockSpec((SG, KP, NLATD * ROWS), lambda g: (g, 0, 0)),
+            pl.BlockSpec((512, 1024), lambda g: (0, 0)),
         ],
         out_specs=[
-            pl.BlockSpec(memory_space=pl.ANY),
-            pl.BlockSpec((SG, 2 * ENTRIES, NLATD * ROWS), lambda g: (g, 0, 0)),
+            pl.BlockSpec((32 * MROWS, 128), lambda g: (0, 0)),
             pl.BlockSpec((SG, 2, NLATD * ROWS, ENTRIES), lambda g: (g, 0, 0, 0)),
         ],
         scratch_shapes=[
+            pltpu.VMEM((NLATD, 2 * SLOTS, 2 * ROWS * CW), BF16),
+            pltpu.VMEM((SLOTS, 2 * ENTRIES, NLATD * ROWS), BF16),
+            pltpu.VMEM((6, NLATD * 24, 128), F32),
+            pltpu.VMEM((2 * SG, NLATD * ROWS, 128), F32),
+            pltpu.VMEM((32 * MROWS, 128), F32),
             pltpu.SemaphoreType.DMA((NLATD,)),
             pltpu.SemaphoreType.DMA((NLATD,)),
             pltpu.SemaphoreType.DMA,
         ],
         out_shape=[
-            jax.ShapeDtypeStruct(spectra.shape, BF16),
-            jax.ShapeDtypeStruct((SLOTS, 2 * ENTRIES, NLATD * ROWS), BF16),
+            jax.ShapeDtypeStruct((32 * MROWS, 128), BF16),
             jax.ShapeDtypeStruct((SLOTS, 2, NLATD * ROWS, ENTRIES), BF16),
         ],
         compiler_params=pltpu.CompilerParams(
             vmem_limit_bytes=VMEM_LIMIT, collective_id=2, has_side_effects=True
         ),
-        name="exchange_out_sort_table",
-    )(spectra, first, legendre)
+        name="outbound_legendre",
+    )(spectra, first, legendre, jnp.asarray(swap_mirror_table()))
 
 
 def opening_kernel(
@@ -778,12 +766,12 @@
     local.start()
     pl.semaphore_wait(barrier, 33)
 
-    def halo(side):
+    def halo(side, row):
         return pltpu.make_async_remote_copy(
-            src_ref=rows_ref.at[pl.ds(side * (HALO + ROWS), HALO)],
-            dst_ref=left_ref if side else right_ref,
-            send_sem=halo_send.at[side],
-            recv_sem=halo_recv.at[side],
+            src_ref=rows_ref.at[side * (HALO + ROWS) + row],
+            dst_ref=(left_ref if side else right_ref).at[row],
+            send_sem=halo_send.at[side, row],
+            recv_sem=halo_recv.at[side, row],
             device_id=partner("lat", rightward if side else leftward),
             device_id_type=pl.DeviceIdType.MESH,
         )
@@ -799,8 +787,9 @@
             device_id_type=pl.DeviceIdType.MESH,
         )
 
-    for side in range(2):
-        halo(side).start()
+    for row in range(HALO):
+        for side in range(2):
+            halo(side, row).start()
 
     def start(k, carry):
         copy(k, 1).start()
@@ -816,8 +805,9 @@
     lax.fori_loop(1, 32, finish, 0)
     local.wait()
     for side in range(2):
-        halo(side).wait_send()
-        halo(side).wait_recv()
+        for row in range(HALO):
+            halo(side, row).wait_send()
+            halo(side, row).wait_recv()
 
 
 def run_opening(rows, by_degree):
@@ -829,8 +819,8 @@
             pltpu.SemaphoreType.DMA((32,)),
             pltpu.SemaphoreType.DMA((32,)),
             pltpu.SemaphoreType.DMA,
-            pltpu.SemaphoreType.DMA((2,)),
-            pltpu.SemaphoreType.DMA((2,)),
+            pltpu.SemaphoreType.DMA((2, HALO)),
+            pltpu.SemaphoreType.DMA((2, HALO)),
         ],
         out_shape=[
             jax.ShapeDtypeStruct((HALO, CW, NLON), BF16),
@@ -840,23 +830,6 @@
         compiler_params=pltpu.CompilerParams(collective_id=0, has_side_effects=True),
         name="opening_exchange",
     )(rows, by_degree)
-
-
-def exchange(kind, collective, x):
-    n = x.shape[0]
-    return pl.pallas_call(
-        functools.partial(exchange_kernel, kind, n),
-        in_specs=[pl.BlockSpec(memory_space=pl.ANY)],
-        out_specs=pl.BlockSpec(memory_space=pl.ANY),
-        scratch_shapes=[
-            pltpu.SemaphoreType.DMA((n,)),
-            pltpu.SemaphoreType.DMA((n,)),
-            pltpu.SemaphoreType.DMA,
-        ],
-        out_shape=jax.ShapeDtypeStruct(x.shape, x.dtype),
-        compiler_params=pltpu.CompilerParams(collective_id=collective, has_side_effects=True),
-        name="exchange_" + kind,
-    )(x)
 
 
 def order_columns(pairing):
@@ -913,10 +886,7 @@
         )
     )
     spectra = jnp.dot(one_hot(sides, L), by_order, preferred_element_type=F32).astype(BF16)
-    incoming, table, turned = run_outbound(
-        spectra.reshape(NLATD, 24, 2 * ROWS * CW), first, legendre
-    )
-    coeffs = run_legendre(first, incoming.reshape(NLATD * 24, 2 * ROWS * CW), table)
+    coeffs, turned = run_outbound(spectra.reshape(NLATD, 24, 2 * ROWS * CW), first, legendre)
     at_owner = lax.all_to_all(
         coeffs.reshape(32, MROWS, 128), ("y", "chan"), split_axis=0, concat_axis=0, tiled=True
     )
@@ -929,8 +899,7 @@
     a_here = jnp.concatenate([a_here, jnp.full((NY, 4), -1, jnp.int32)], axis=1).reshape(1, NY * 16)
     a_here = jnp.broadcast_to(a_here, (2, NY * 16)).reshape(128, 1)
     mixed = run_mix(owner, at_owner, weights, a_here)
-    returned = exchange("own", 1, mixed)
-    spectrum, homeward = run_inverse(first, returned.reshape(32 * MROWS, 128), turned)
+    spectrum, homeward = run_inverse(first, mixed.reshape(32 * MROWS, 128), turned)
     spectrum = jnp.transpose(spectrum.reshape(SLOTS, 2, CW, KP), (0, 3, 1, 2))
     homeward = homeward.reshape(NLATD * 24, 2 * ROWS * CW)
     filtered = jnp.dot(

time: 262 us -> 257 us (0.981)
  Pallas kernels: 203 us -> 196 us
    pallas_call x2 -> x0, Pallas kernels: 34.9 us -> none  [the longest x1 22.8 us: exchange(): pl.pallas_call(functools.partial(exchange_kernel, kind, n), in_specs=[pl....]
    pallas_call x1, Pallas kernels: 6.16 us -> 25.6 us  [run_mix(): pl.pallas_call(mix_kernel, in_specs=[pl.BlockSpec(memory_space=pltpu.SMEM...]
    pallas_call x1, Pallas kernels: 48.2 us -> 55.9 us  [run_outbound(): pl.pallas_call(outbound_kernel, grid=(NSG,), in_specs=[pl.BlockSpec(memor...]
  transfers between devices with their start and end apart: 2 -> 2, of which waited for: 0 -> 0; matrix products, arithmetic and copies ran while one was open for 8% -> 9% of each run, Pallas kernels for 26% -> 25%
where the time goes in v1:
time: 257 us
  Pallas kernels  196 us (76%)
  matrix products  22.6 us (9%)
  between operations  15.7 us (6%)
  local copies, waits for them, and re-layouts  11 us (4%)
  starting transfers between devices  7.06 us (3%)
  other arithmetic  4.43 us (2%)
    pallas_call x1, Pallas kernels, run_outbound(): pl.pallas_call(outbound_kernel, grid=(NSG,), in_specs=[pl.BlockSpec(memor...  55.9 us
    pallas_call x1, Pallas kernels, run_inverse(): pl.pallas_call(inverse_kernel, grid=(NSG,), in_specs=[pl.BlockSpec(memory...  39.1 us
    pallas_call x1, Pallas kernels, run_tail(): pl.pallas_call(tail_kernel, in_specs=[pl.BlockSpec(memory_space=pl.ANY)]...  33.2 us
    pallas_call x1, Pallas kernels, run_opening(): pl.pallas_call(opening_kernel, in_specs=[pl.BlockSpec(memory_space=pl.ANY...  29.5 us
    pallas_call x1, Pallas kernels, run_mix(): pl.pallas_call(mix_kernel, in_specs=[pl.BlockSpec(memory_space=pltpu.SMEM...  25.6 us
    dot_general x6, matrix products, dot_nt(): lax.dot_general(a, b, (((1,), (1,)), ((), ())), preferred_element_type=F32)  16.9 us
    pallas_call x1, Pallas kernels, run_weights(): pl.pallas_call(weights_kernel, grid=(NZ // 2,), in_specs=[pl.BlockSpec((2...  8.24 us
    all_to_all x1, starting transfers between devices, per_device(): lax.all_to_all(coeffs.reshape(32, MROWS, 128), ('y', 'chan'), split_axis=...  7.02 us
  transfers between devices with their start and end apart: 2, of which 0 were waited for; matrix products, arithmetic and copies ran while one was open for 9% of the time, Pallas kernels for 25%

profile of v1, /device:TPU:1, one launch (start us, length us, event | category | flops | bytes accessed | tf_op | source)
XLA Modules:
  0.0 257.0 jit_solution(4526507767959834833)
XLA Ops:
  7.2 0.0 all-gather.3.cloned.1.call-start
  7.2 1.3 fusion.17
  9.9 1.9 select_bitcast_fusion
  11.8 1.8 pad_dynamic-slice_fusion.1.rows_ref
  13.6 1.3 convolution_convert_fusion.5
  14.9 29.5 %opening_exchange.1 = (bf16[6,32,1440]{2,1,0:T(8,128)(2,1)}, bf16[6,32,1440]{2,1,0:T(8,128)(2,1)}, bf16[32,24,256]{2,1,0:T(8,128)(2,1)}) custom-call(bf16[24,32,1440]{2,1,0:T(8,128)(2,1)} %pad_dynamic-slice_fusion.1.rows_ref, bf16[32,24,256]{2,1,0:T(8,128)(2,1)} %bitcast.58), custom_call_target="tpu_custom_call" | custom-call | tf_op jit(solution)/shard_map/opening_exchange/pallas_call | solution.py:814
  44.4 1.7 fusion.9
  46.1 0.3 copy-done.11
  46.4 1.3 fusion.8
  47.7 0.5 copy-done.10
  48.2 1.3 fusion.7
  49.5 0.1 pad_maximum_fusion
  49.6 0.6 copy-done.7
  50.2 0.1 reshape.108
  50.3 0.1 copy.31
  50.4 0.1 copy.32
  50.5 0.1 ge.29
  50.6 0.1 copy.30
  50.7 0.1 copy.33
  50.8 0.1 select_n.50
  50.9 0.6 dynamic_slice.10.first_ref
  51.5 2.2 fusion.6
  53.7 55.9 %outbound_legendre.1 = (bf16[5120,128]{1,0:T(8,128)(2,1)}, bf16[12,2,384,416]{3,2,1,0:T(8,128)(2,1)}) custom-call(bf16[32,24,768]{2,1,0:T(8,128)(2,1)} %bitcast.64, s32[12]{0:T(128)} %dynamic_slice.10.first_ref, bf16[12,721,384]{2,1,0:T(8,128)(2,1)} %leg_ref.1, bf16[512,1024]{1,0:T(8,128)(2,1)} %constant.84.clone.swap_ref), custom_call_target="tpu_custom_call" | custom-call | tf_op jit(solution)/shard_map/outbound_legendre/pallas_call | solution.py:718
  109.7 7.0 %all-to-all-start = ((bf16[32,160,128]{2,1,0:T(8,128)(2,1)}), bf16[32,160,128]{2,1,0:T(8,128)(2,1)S(1)}, u32[]{:S(2)}, u32[]{:S(2)}) async-start(bf16[32,160,128]{2,1,0:T(8,128)(2,1)} %bitcast.59), calls=%async_computation | async-start | bytes 2621440 | tf_op jit(solution)/shard_map/all_to_all | solution.py:890
  116.7 0.1 concatenate.24
  116.8 0.1 ge.30
  117.0 0.1 reshape.116
  117.1 0.1 copy.35
  117.2 0.1 copy.36
  117.3 0.1 copy.34
  117.4 0.1 copy.37
  117.5 0.2 eq.31
  117.7 0.1 broadcast_in_dim.54
  117.8 0.8 reshape.182.a_ref
  118.6 0.7 pad_add_fusion.place_ref
  119.3 5.2 %fusion = bf16[1536,768]{0,1:T(8,128)(2,1)} fusion(bf16[1536,720]{1,0:T(8,128)(2,1)} %constant.79.clone, s32[768]{0:T(1024)S(1)} %eq.31), kind=kOutput, calls=%fused_computation.5 | convolution fusion | flops 1700425728 | bytes 4574208 | tf_op jit(solution)/shard_map/dot_general | solution.py:845
  124.5 3.4 %fusion.1 = bf16[1536,768]{0,1:T(8,128)(2,1)} fusion(bf16[1536,720]{1,0:T(8,128)(2,1)S(1)} %copy-done.9, s32[768]{0:T(1024)S(1)} %eq.31), kind=kOutput, calls=%fused_computation.6 | convolution fusion | flops 1700425728 | bytes 4574208 | tf_op jit(solution)/shard_map/dot_general | solution.py:845
  127.9 4.4 %fusion.4 = bf16[1536,384]{0,1:T(8,128)(2,1)S(1)} fusion(bf16[384,1440]{1,0:T(8,128)(2,1)S(1)} %bitcast.62, bf16[1536,1440]{1,0:T(8,128)(2,1)} %constant.81.clone), kind=kOutput, calls=%fused_computation.10 | convolution fusion | flops 1699282944 | bytes 6709248 | tf_op jit(solution)/shard_map/dot_general | solution.py:845
  132.4 8.2 %unpack_weights.1 = bf16[24,4,8,8,256]{4,3,2,1,0:T(8,128)(2,1)} custom-call(bf16[8,32,24,256]{3,2,1,0:T(8,128)(2,1)} %bitcast.66, bf16[512,512]{1,0:T(8,128)(2,1)} %constant.78.clone.swap_ref), custom_call_target="tpu_custom_call" | custom-call | flops 4000000000 | bytes 6000000 | tf_op jit(solution)/shard_map/unpack_weights/pallas_call | solution.py:169
  140.6 1.1 copy-done.2
  141.7 25.6 %mix_degrees.1 = bf16[32,160,128]{2,1,0:T(8,128)(2,1)} custom-call(s32[1]{0:T(128)} %bitcast.21.owner_ref, bf16[32,160,128]{2,1,0:T(8,128)(2,1)} %copy-done.2, bf16[24,256,256]{2,1,0:T(8,128)(2,1)} %bitcast.56, s32[128,1]{1,0:T(8,128)} %reshape.182.a_ref, bf16[512,512]{1,0:T(8,128)(2,1)} %constant.78.clone.swap_ref), custom_call_target="tpu_custom_call" | custom-call | tf_op jit(solution)/shard_map/mix_degrees/pallas_call | solution.py:280
  167.3 39.1 %legendre_inverse_home.1 = (bf16[12,64,721]{2,1,0:T(8,128)(2,1)}, bf16[3,32,8,768]{3,2,1,0:T(8,128)(2,1)}) custom-call(s32[12]{0:T(128)} %dynamic_slice.10.first_ref, bf16[5120,128]{1,0:T(8,128)(2,1)} %bitcast.54, bf16[12,2,384,416]{3,2,1,0:T(8,128)(2,1)} %get-tuple-element.25.turned_ref, bf16[512,512]{1,0:T(8,128)(2,1)} %constant.78.clone.swap_ref), custom_call_target="tpu_custom_call" | custom-call | tf_op jit(solution)/shard_map/legendre_inverse_home/pallas_call | solution.py:403
  206.5 2.3 fusion.14
  208.8 1.1 fusion.3
  210.0 1.4 copy.41
  211.4 33.2 %pointwise_tail.1 = (bf16[12,180,256]{2,1,0:T(8,128)(2,1)}, bf16[6,180,256]{2,1,0:T(8,128)(2,1)}, bf16[6,180,256]{2,1,0:T(8,128)(2,1)}) custom-call(bf16[8,192,384]{2,1,0:T(8,128)(2,1)} %bitcast.55, bf16[256,512]{1,0:T(8,128)(2,1)} %w_in_ref.1, bf16[512,256]{1,0:T(8,128)(2,1)} %w_out_ref.1, bf16[512,512]{1,0:T(8,128)(2,1)} %constant.78.clone.swap_ref), custom_call_target="tpu_custom_call" | custom-call | tf_op jit(solution)/shard_map/pointwise_tail/pallas_call | solution.py:541
  244.7 4.5 %assemble_bands.1 = bf16[4320,256]{1,0:T(8,128)(2,1)} custom-call(s32[2]{0:T(128)} %pad_add_fusion.place_ref, bf16[6,180,256]{2,1,0:T(8,128)(2,1)} %get-tuple-element.28.left_ref, bf16[12,180,256]{2,1,0:T(8,128)(2,1)} %get-tuple-element.29.own_ref, bf16[6,180,256]{2,1,0:T(8,128)(2,1)} %get-tuple-element.30.right_ref), custom_call_target="tpu_custom_call" | custom-call | tf_op jit(solution)/shard_map/assemble_bands/pallas_call | solution.py:586
  249.2 1.0 copy.45
  (36 shorter events, 0.2 us)
Async XLA Ops:
  7.2 6.4 %copy-start = (bf16[720,8,32]{0,2,1:T(8,128)(2,1)S(1)}, bf16[720,8,32]{0,2,1:T(8,128)(2,1)}, u32[]{:S(2)}) copy-start(bf16[720,8,32]{0,2,1:T(8,128)(2,1)} %param.22) | copy-start | bytes 1105924
  7.2 125.2 %all-gather.3.cloned.1.call-start = ((), (), s32[]{:S(2)}) async-start(), calls=%async_computation.1 | async-start | bytes 3538944 | tf_op jit(solution)/shard_map/all_gather | solution.py:870
  11.8 1.8 copy-start.6
  44.4 2.0 copy-start.11
  46.1 1.6 copy-start.3
  46.4 1.8 copy-start.10
  49.5 0.7 copy-start.7
  109.7 30.9 %all-to-all-start = ((bf16[32,160,128]{2,1,0:T(8,128)(2,1)}), bf16[32,160,128]{2,1,0:T(8,128)(2,1)S(1)}, u32[]{:S(2)}, u32[]{:S(2)}) async-start(bf16[32,160,128]{2,1,0:T(8,128)(2,1)} %bitcast.59), calls=%async_computation | async-start | bytes 2621440 | tf_op jit(solution)/shard_map/all_to_all | solution.py:890
  119.3 5.2 %copy-start.9 = (bf16[1536,720]{1,0:T(8,128)(2,1)S(1)}, bf16[1536,720]{1,0:T(8,128)(2,1)}, u32[]{:S(2)}) copy-start(bf16[1536,720]{1,0:T(8,128)(2,1)} %constant.80.clone) | copy-start | bytes 6635524
  124.5 3.4 %copy-start.4 = (bf16[12,32,1440]{2,1,0:T(8,128)(2,1)S(1)}, bf16[12,32,1440]{2,1,0:T(8,128)(2,1)}, u32[]{:S(2)}) copy-start(bf16[12,32,1440]{2,1,0:T(8,128)(2,1)} %copy-done.3) | copy-start | bytes 3317764
  140.6 1.1 copy-start.2
  167.3 39.2 %copy-start.12 = (bf16[1536,768]{0,1:T(8,128)(2,1)S(1)}, bf16[1536,768]{0,1:T(8,128)(2,1)}, u32[]{:S(2)}) copy-start(bf16[1536,768]{0,1:T(8,128)(2,1)} %fusion) | copy-start | bytes 7077892
  206.4 2.4 copy-start.8
  206.5 2.4 copy-start.13
  244.6 4.5 %copy-start.5 = (bf16[12,64,721]{2,1,0:T(8,128)(2,1)S(1)}, bf16[12,64,721]{2,1,0:T(8,128)(2,1)}, u32[]{:S(2)}) copy-start(bf16[12,64,721]{2,1,0:T(8,128)(2,1)} %get-tuple-element.31) | copy-start | bytes 3322372
  244.6 5.6 %copy-start.1 = (bf16[720,8,32]{0,2,1:T(8,128)(2,1)S(1)}, bf16[720,8,32]{0,2,1:T(8,128)(2,1)}, u32[]{:S(2)}) copy-start(bf16[720,8,32]{0,2,1:T(8,128)(2,1)} %param.22) | copy-start | bytes 1105924
Sparse Core Ops, SparseCore 0:
  44.5 66.5 all-gather.2

commit v2 on v1

--- a/solution.py
+++ b/solution.py
@@ -647,7 +647,8 @@
 
 
 def outbound_kernel(
-    x_ref, first_ref, leg_ref, swap_ref, coeff_ref, turned_ref,
+    x_ref, first_ref, leg_ref, swap_ref, wave_re_ref, wave_im_ref, home_ref,
+    coeff_ref, turned_ref, inverse_re_ref, inverse_im_ref,
     arrived, table, scr_f, scr_r, scr_o, send_sem, recv_sem, local_sem,
 ):
     group = pl.program_id(0)
@@ -687,6 +688,12 @@
         table[group * SG + ss, ENTRIES:] = y.astype(BF16)
         turned_ref[ss, 0] = jnp.transpose(x).astype(BF16)
         turned_ref[ss, 1] = jnp.transpose(y).astype(BF16)
+    inverse_re_ref[...] = jnp.dot(
+        wave_re_ref[...], home_ref[...], preferred_element_type=F32
+    ).astype(BF16)
+    inverse_im_ref[...] = jnp.dot(
+        wave_im_ref[...], home_ref[...], preferred_element_type=F32
+    ).astype(BF16)
 
     @pl.when(group == NSG - 1)
     def _():
@@ -714,7 +721,8 @@
         coeff_ref[...] = scr_o[...].astype(BF16)
 
 
-def run_outbound(spectra, first, legendre):
+def run_outbound(spectra, first, legendre, home):
+    waves = inverse_table()
     return pl.pallas_call(
         outbound_kernel,
         grid=(NSG,),
@@ -723,10 +731,15 @@
             pl.BlockSpec(memory_space=pltpu.SMEM),
             pl.BlockSpec((SG, KP, NLATD * ROWS), lambda g: (g, 0, 0)),
             pl.BlockSpec((512, 1024), lambda g: (0, 0)),
+            pl.BlockSpec((NPADDED // NSG, L), lambda g: (g, 0)),
+            pl.BlockSpec((NPADDED // NSG, L), lambda g: (g, 0)),
+            pl.BlockSpec((L, NLATD * 24), lambda g: (0, 0)),
         ],
         out_specs=[
             pl.BlockSpec((32 * MROWS, 128), lambda g: (0, 0)),
             pl.BlockSpec((SG, 2, NLATD * ROWS, ENTRIES), lambda g: (g, 0, 0, 0)),
+            pl.BlockSpec((NPADDED // NSG, NLATD * 24), lambda g: (g, 0)),
+            pl.BlockSpec((NPADDED // NSG, NLATD * 24), lambda g: (g, 0)),
         ],
         scratch_shapes=[
             pltpu.VMEM((NLATD, 2 * SLOTS, 2 * ROWS * CW), BF16),
@@ -741,12 +754,22 @@
         out_shape=[
             jax.ShapeDtypeStruct((32 * MROWS, 128), BF16),
             jax.ShapeDtypeStruct((SLOTS, 2, NLATD * ROWS, ENTRIES), BF16),
+            jax.ShapeDtypeStruct((NPADDED, NLATD * 24), BF16),
+            jax.ShapeDtypeStruct((NPADDED, NLATD * 24), BF16),
         ],
         compiler_params=pltpu.CompilerParams(
             vmem_limit_bytes=VMEM_LIMIT, collective_id=2, has_side_effects=True
         ),
         name="outbound_legendre",
-    )(spectra, first, legendre, jnp.asarray(swap_mirror_table()))
+    )(
+        spectra,
+        first,
+        legendre,
+        jnp.asarray(swap_mirror_table()),
+        jnp.asarray(waves[:, :L]),
+        jnp.asarray(waves[:, L:]),
+        home,
+    )
 
 
 def opening_kernel(
@@ -872,10 +895,8 @@
     weights = weights.reshape(2 * JO, 256, 256)
 
     sides = order_columns(pairing)
-    home = one_hot(sides.reshape(NLATD, 2, NSG, SG).transpose(2, 0, 1, 3), L)
-    waves_back = inverse_table()
-    inverse_re = dot_nt(jnp.asarray(waves_back[:, :L]), home).astype(BF16)
-    inverse_im = dot_nt(jnp.asarray(waves_back[:, L:]), home).astype(BF16)
+    home = sides.reshape(NLATD, 2, NSG, SG).transpose(2, 0, 1, 3).reshape(-1)
+    home = (jnp.arange(L, dtype=jnp.int32)[:, None] == home[None, :]).astype(BF16)
     padded = dot_nt(jnp.asarray(pad_rows()), xt).astype(BF16)
 
     waves = forward_table()
@@ -886,13 +907,13 @@
         )
     )
     spectra = jnp.dot(one_hot(sides, L), by_order, preferred_element_type=F32).astype(BF16)
-    coeffs, turned = run_outbound(spectra.reshape(NLATD, 24, 2 * ROWS * CW), first, legendre)
+    coeffs, turned, inverse_re, inverse_im = run_outbound(
+        spectra.reshape(NLATD, 24, 2 * ROWS * CW), first, legendre, home
+    )
     at_owner = lax.all_to_all(
         coeffs.reshape(32, MROWS, 128), ("y", "chan"), split_axis=0, concat_axis=0, tiled=True
     )
-    at_owner, weights, inverse_re, inverse_im, padded = lax.optimization_barrier(
-        (at_owner, weights, inverse_re, inverse_im, padded)
-    )
+    at_owner, weights, padded = lax.optimization_barrier((at_owner, weights, padded))
     owner = (lax.axis_index("y") * NCH + chan).reshape(1)
     z = lax.axis_index("z")
     a_here = lax.dynamic_slice_in_dim(pairing.reshape(NY, NZ, SLOTS), z, 1, axis=1)[:, 0]

time: 257 us -> 255 us (level)
  matrix products: 22.6 us -> 16.3 us
  waiting for transfers between devices: 0.04 us -> 3.91 us
    dot_general x6 -> x4, matrix products: 16.9 us -> 10.6 us  [dot_nt(): lax.dot_general(a, b, (((1,), (1,)), ((), ())), preferred_element_type=F32)]
    all_to_all x1, waiting for transfers between devices: 0.01 us -> 3.89 us  [per_device(): lax.all_to_all(coeffs.reshape(32, MROWS, 128), ('y', 'chan'), split_axis=...]
  transfers between devices with their start and end apart: 2 -> 2, of which waited for: 0 -> 1; matrix products, arithmetic and copies ran while one was open for 9% -> 7% of each run, Pallas kernels for 25% -> 26%
where the time goes in v2:
time: 255 us; the launch traced here: 254 us
  Pallas kernels  195 us (76%)
  matrix products  16.3 us (6%)
  between operations  15.6 us (6%)
  local copies, waits for them, and re-layouts  10.6 us (4%)
  starting transfers between devices  7.46 us (3%)
  other arithmetic  5.8 us (2%)
  waiting for transfers between devices  3.91 us (2%)
    pallas_call x1, Pallas kernels, run_outbound(): pl.pallas_call(outbound_kernel, grid=(NSG,), in_specs=[pl.BlockSpec(memor...  57 us
    pallas_call x1, Pallas kernels, run_inverse(): pl.pallas_call(inverse_kernel, grid=(NSG,), in_specs=[pl.BlockSpec(memory...  39.1 us
    pallas_call x1, Pallas kernels, run_tail(): pl.pallas_call(tail_kernel, in_specs=[pl.BlockSpec(memory_space=pl.ANY)]...  32.1 us
    pallas_call x1, Pallas kernels, run_opening(): pl.pallas_call(opening_kernel, in_specs=[pl.BlockSpec(memory_space=pl.ANY...  29.5 us
    pallas_call x1, Pallas kernels, run_mix(): pl.pallas_call(mix_kernel, in_specs=[pl.BlockSpec(memory_space=pltpu.SMEM...  24.3 us
    dot_general x4, matrix products, dot_nt(): lax.dot_general(a, b, (((1,), (1,)), ((), ())), preferred_element_type=F32)  10.6 us
    pallas_call x1, Pallas kernels, run_weights(): pl.pallas_call(weights_kernel, grid=(NZ // 2,), in_specs=[pl.BlockSpec((2...  8.23 us
    all_to_all x1, starting transfers between devices, per_device(): lax.all_to_all(coeffs.reshape(32, MROWS, 128), ('y', 'chan'), split_axis=...  7.42 us
  transfers between devices with their start and end apart: 2, of which 1 were waited for; matrix products, arithmetic and copies ran while one was open for 7% of the time, Pallas kernels for 26%

profile of v2, /device:TPU:1, one launch (start us, length us, event | category | flops | bytes accessed | tf_op | source)
XLA Modules:
  0.0 254.2 jit_solution(775334712765834715)
XLA Ops:
  7.2 0.0 all-gather.3.cloned.1.call-start
  7.2 1.4 fusion.14
  9.9 2.5 convolution_convert_fusion.3
  12.5 1.9 select_bitcast_fusion
  14.4 1.8 pad_dynamic-slice_fusion.1.rows_ref
  16.2 29.5 %opening_exchange.1 = (bf16[6,32,1440]{2,1,0:T(8,128)(2,1)}, bf16[6,32,1440]{2,1,0:T(8,128)(2,1)}, bf16[32,24,256]{2,1,0:T(8,128)(2,1)}) custom-call(bf16[24,32,1440]{2,1,0:T(8,128)(2,1)} %pad_dynamic-slice_fusion.1.rows_ref, bf16[32,24,256]{2,1,0:T(8,128)(2,1)} %bitcast.52), custom_call_target="tpu_custom_call" | custom-call | tf_op jit(solution)/shard_map/opening_exchange/pallas_call | solution.py:837
  45.8 0.1 ge.29
  45.9 0.1 ge.30
  46.0 0.1 reshape.108
  46.1 0.1 concatenate.24
  46.2 0.6 dynamic_slice.10.first_ref
  46.8 0.1 copy.30
  46.9 0.1 copy.34
  47.0 0.1 copy.31
  47.1 0.1 copy.32
  47.2 0.1 copy.33
  47.3 0.1 select_n.50
  47.4 0.1 copy.35
  47.6 0.1 copy.36
  47.7 0.1 copy.37
  47.8 0.2 eq.32
  48.0 1.7 fusion.8
  49.7 0.3 copy-done.11
  50.0 1.3 fusion.7
  51.3 0.4 copy-done.10
  51.7 1.3 fusion.6
  53.1 0.1 pad_maximum_fusion
  53.2 1.4 fusion.4.home_ref
  54.6 2.2 fusion.5
  56.8 57.0 %outbound_legendre.1 = (bf16[5120,128]{1,0:T(8,128)(2,1)}, bf16[12,2,384,416]{3,2,1,0:T(8,128)(2,1)}, bf16[1536,768]{1,0:T(8,128)(2,1)}, bf16[1536,768]{1,0:T(8,128)(2,1)}) custom-call(bf16[32,24,768]{2,1,0:T(8,128)(2,1)} %bitcast.54, s32[12]{0:T(128)} %dynamic_slice.10.first_ref, bf16[12,721,384]{2,1,0:T(8,128)(2,1)} %leg_ref.1, ...), custom_call_target="tpu_custom_call" | custom-call | tf_op jit(solution)/shard_map/outbound_legendre/pallas_call | solution.py:726
  113.9 7.4 %all-to-all-start = ((bf16[32,160,128]{2,1,0:T(8,128)(2,1)}), bf16[32,160,128]{2,1,0:T(8,128)(2,1)S(1)}, u32[]{:S(2)}, u32[]{:S(2)}) async-start(bf16[32,160,128]{2,1,0:T(8,128)(2,1)} %bitcast.53), calls=%async_computation | async-start | bytes 2621440 | tf_op jit(solution)/shard_map/all_to_all | solution.py:913
  121.3 0.1 reshape.116
  121.4 0.1 broadcast_in_dim.54
  121.5 0.8 reshape.182.a_ref
  122.3 0.6 pad_add_fusion.place_ref
  122.9 5.4 %fusion.2 = bf16[1536,384]{0,1:T(8,128)(2,1)} fusion(bf16[384,1440]{1,0:T(8,128)(2,1)S(1)} %bitcast.57, bf16[1536,1440]{1,0:T(8,128)(2,1)} %constant.79.clone), kind=kOutput, calls=%fused_computation.6 | convolution fusion | flops 1699282944 | bytes 6709248 | tf_op jit(solution)/shard_map/dot_general | solution.py:868
  128.3 8.2 %unpack_weights.1 = bf16[24,4,8,8,256]{4,3,2,1,0:T(8,128)(2,1)} custom-call(bf16[8,32,24,256]{3,2,1,0:T(8,128)(2,1)} %bitcast.60, bf16[512,512]{1,0:T(8,128)(2,1)} %constant.78.clone.swap_ref), custom_call_target="tpu_custom_call" | custom-call | flops 4000000000 | bytes 6000000 | tf_op jit(solution)/shard_map/unpack_weights/pallas_call | solution.py:169
  136.5 3.9 %all-to-all-done.d_ref = bf16[32,160,128]{2,1,0:T(8,128)(2,1)S(1)} async-done(((bf16[32,160,128]{2,1,0:T(8,128)(2,1)}), bf16[32,160,128]{2,1,0:T(8,128)(2,1)S(1)}, u32[]{:S(2)}, u32[]{:S(2)}) %all-to-all-start) | async-done | bytes 1310752 | tf_op jit(solution)/shard_map/all_to_all | solution.py:913
  140.4 1.1 copy-done.2
  141.5 24.3 %mix_degrees.1 = bf16[32,160,128]{2,1,0:T(8,128)(2,1)} custom-call(s32[1]{0:T(128)} %bitcast.19.owner_ref, bf16[32,160,128]{2,1,0:T(8,128)(2,1)} %copy-done.2, bf16[24,256,256]{2,1,0:T(8,128)(2,1)} %bitcast.50, s32[128,1]{1,0:T(8,128)} %reshape.182.a_ref, bf16[512,512]{1,0:T(8,128)(2,1)} %constant.78.clone.swap_ref), custom_call_target="tpu_custom_call" | custom-call | tf_op jit(solution)/shard_map/mix_degrees/pallas_call | solution.py:280
  165.7 39.1 %legendre_inverse_home.1 = (bf16[12,64,721]{2,1,0:T(8,128)(2,1)}, bf16[3,32,8,768]{3,2,1,0:T(8,128)(2,1)}) custom-call(s32[12]{0:T(128)} %dynamic_slice.10.first_ref, bf16[5120,128]{1,0:T(8,128)(2,1)} %bitcast.48, bf16[12,2,384,416]{3,2,1,0:T(8,128)(2,1)} %get-tuple-element.25.turned_ref, bf16[512,512]{1,0:T(8,128)(2,1)} %constant.78.clone.swap_ref), custom_call_target="tpu_custom_call" | custom-call | tf_op jit(solution)/shard_map/legendre_inverse_home/pallas_call | solution.py:403
  204.9 2.3 fusion.11
  207.2 0.1 copy-done.12
  207.4 1.2 fusion.1
  208.5 1.4 copy.41
  209.9 32.1 %pointwise_tail.1 = (bf16[12,180,256]{2,1,0:T(8,128)(2,1)}, bf16[6,180,256]{2,1,0:T(8,128)(2,1)}, bf16[6,180,256]{2,1,0:T(8,128)(2,1)}) custom-call(bf16[8,192,384]{2,1,0:T(8,128)(2,1)} %bitcast.49, bf16[256,512]{1,0:T(8,128)(2,1)} %w_in_ref.1, bf16[512,256]{1,0:T(8,128)(2,1)} %w_out_ref.1, bf16[512,512]{1,0:T(8,128)(2,1)} %constant.78.clone.swap_ref), custom_call_target="tpu_custom_call" | custom-call | tf_op jit(solution)/shard_map/pointwise_tail/pallas_call | solution.py:541
  242.0 4.3 %assemble_bands.1 = bf16[4320,256]{1,0:T(8,128)(2,1)} custom-call(s32[2]{0:T(128)} %pad_add_fusion.place_ref, bf16[6,180,256]{2,1,0:T(8,128)(2,1)} %get-tuple-element.28.left_ref, bf16[12,180,256]{2,1,0:T(8,128)(2,1)} %get-tuple-element.29.own_ref, bf16[6,180,256]{2,1,0:T(8,128)(2,1)} %get-tuple-element.30.right_ref), custom_call_target="tpu_custom_call" | custom-call | tf_op jit(solution)/shard_map/assemble_bands/pallas_call | solution.py:586
  246.3 1.0 copy.45
  (33 shorter events, 0.2 us)
Async XLA Ops:
  7.2 2.8 %copy-start = (bf16[720,8,32]{0,2,1:T(8,128)(2,1)S(1)}, bf16[720,8,32]{0,2,1:T(8,128)(2,1)}, u32[]{:S(2)}) copy-start(bf16[720,8,32]{0,2,1:T(8,128)(2,1)} %param.22) | copy-start | bytes 1105924
  7.2 121.1 %all-gather.3.cloned.1.call-start = ((), (), s32[]{:S(2)}) async-start(), calls=%async_computation.1 | async-start | bytes 3538944 | tf_op jit(solution)/shard_map/all_gather | solution.py:893
  16.2 29.6 %copy-start.6 = (s32[384]{0:T(512)S(1)}, s32[384]{0:T(512)}, u32[]{:S(2)}) copy-start(s32[384]{0:T(512)} %param.19) | copy-start | bytes 4612
  48.0 2.0 copy-start.11
  49.7 1.6 copy-start.3
  50.0 1.8 copy-start.10
  113.8 9.1 %copy-start.4 = (bf16[12,32,1440]{2,1,0:T(8,128)(2,1)S(1)}, bf16[12,32,1440]{2,1,0:T(8,128)(2,1)}, u32[]{:S(2)}) copy-start(bf16[12,32,1440]{2,1,0:T(8,128)(2,1)} %copy-done.3) | copy-start | bytes 3317764
  113.9 26.5 %all-to-all-start = ((bf16[32,160,128]{2,1,0:T(8,128)(2,1)}), bf16[32,160,128]{2,1,0:T(8,128)(2,1)S(1)}, u32[]{:S(2)}, u32[]{:S(2)}) async-start(bf16[32,160,128]{2,1,0:T(8,128)(2,1)} %bitcast.53), calls=%async_computation | async-start | bytes 2621440 | tf_op jit(solution)/shard_map/all_to_all | solution.py:913
  140.4 1.1 copy-start.2
  165.7 39.1 %copy-start.8 = (bf16[1536,768]{1,0:T(8,128)(2,1)S(1)}, bf16[1536,768]{1,0:T(8,128)(2,1)}, u32[]{:S(2)}) copy-start(bf16[1536,768]{1,0:T(8,128)(2,1)} %get-tuple-element.22) | copy-start | bytes 7077892
  204.8 2.4 copy-start.7
  204.9 2.4 copy-start.9
  204.9 2.5 copy-start.12
  242.0 4.3 %copy-start.5 = (bf16[12,64,721]{2,1,0:T(8,128)(2,1)S(1)}, bf16[12,64,721]{2,1,0:T(8,128)(2,1)}, u32[]{:S(2)}) copy-start(bf16[12,64,721]{2,1,0:T(8,128)(2,1)} %get-tuple-element.31) | copy-start | bytes 3322372
  242.0 5.3 %copy-start.1 = (bf16[720,8,32]{0,2,1:T(8,128)(2,1)S(1)}, bf16[720,8,32]{0,2,1:T(8,128)(2,1)}, u32[]{:S(2)}) copy-start(bf16[720,8,32]{0,2,1:T(8,128)(2,1)} %param.22) | copy-start | bytes 1105924
Sparse Core Ops, SparseCore 0:
  45.9 66.5 all-gather.2

commit v3 on v2

--- a/solution.py
+++ b/solution.py
@@ -878,11 +878,11 @@
     cap = grid_in.shape[0]
 
     rows = jnp.transpose(grid_in, (0, 2, 1))
-    valid = (jnp.arange(cap, dtype=jnp.int32) < length)[:, None, None]
-    rows = jnp.where(valid, rows, jnp.zeros((), BF16))
     shift = me * ROWS - HALO - start
     rows = jnp.concatenate([jnp.zeros((12, CW, NLON), BF16), rows], axis=0)
     virt = lax.dynamic_slice_in_dim(rows, 12 + shift, cap, axis=0)
+    stored = jnp.arange(cap, dtype=jnp.int32) + shift
+    virt = jnp.where(((stored >= 0) & (stored < length))[:, None, None], virt, jnp.zeros((), BF16))
     own = virt[HALO : HALO + ROWS]
     by_degree = dot_nt(
         jnp.asarray(degree_order()),

time: 255 us -> 254 us (level)
  no operation moved by 1% of the time
where the time goes in v3:
time: 254 us; the launch traced here: 253 us
  Pallas kernels  194 us (76%)
  matrix products  16.3 us (6%)
  between operations  15.6 us (6%)
  local copies, waits for them, and re-layouts  8.76 us (3%)
  starting transfers between devices  7.18 us (3%)
  other arithmetic  7.04 us (3%)
  waiting for transfers between devices  3.89 us (2%)
    pallas_call x1, Pallas kernels, run_outbound(): pl.pallas_call(outbound_kernel, grid=(NSG,), in_specs=[pl.BlockSpec(memor...  57.1 us
    pallas_call x1, Pallas kernels, run_inverse(): pl.pallas_call(inverse_kernel, grid=(NSG,), in_specs=[pl.BlockSpec(memory...  39.2 us
    pallas_call x1, Pallas kernels, run_tail(): pl.pallas_call(tail_kernel, in_specs=[pl.BlockSpec(memory_space=pl.ANY)]...  32 us
    pallas_call x1, Pallas kernels, run_opening(): pl.pallas_call(opening_kernel, in_specs=[pl.BlockSpec(memory_space=pl.ANY...  29.4 us
    pallas_call x1, Pallas kernels, run_mix(): pl.pallas_call(mix_kernel, in_specs=[pl.BlockSpec(memory_space=pltpu.SMEM...  24.3 us
    dot_general x4, matrix products, dot_nt(): lax.dot_general(a, b, (((1,), (1,)), ((), ())), preferred_element_type=F32)  10.6 us
    pallas_call x1, Pallas kernels, run_weights(): pl.pallas_call(weights_kernel, grid=(NZ // 2,), in_specs=[pl.BlockSpec((2...  8.23 us
    all_to_all x1, starting transfers between devices, per_device(): lax.all_to_all(coeffs.reshape(32, MROWS, 128), ('y', 'chan'), split_axis=...  7.14 us
  transfers between devices with their start and end apart: 2, of which 1 were waited for; matrix products, arithmetic and copies ran while one was open for 7% of the time, Pallas kernels for 26%

profile of v3, /device:TPU:1, one launch (start us, length us, event | category | flops | bytes accessed | tf_op | source)
XLA Modules:
  0.0 253.3 jit_solution(9377395816214192624)
XLA Ops:
  7.2 0.0 all-gather.3.cloned.1.call-start
  7.2 1.3 fusion.14
  9.9 2.5 convolution_convert_fusion.3
  12.4 3.3 %fusion.3.rows_ref = bf16[24,32,1440]{2,1,0:T(8,128)(2,1)} fusion(s32[]{:T(128)S(6)} %select_n.48, bf16[24,32,1440]{2,1,0:T(8,128)(2,1)} %bitcast.50, pred[24]{0:T(512)(128)(4,1)S(1)} %compare_and_fusion), kind=kLoop, calls=%fused_computation.6 | loop fusion | flops 1105920 | bytes 4423708 | tf_op jit(solution)/shard_map/jit(_where)/select_n | solution.py:885
  15.7 29.4 %opening_exchange.1 = (bf16[6,32,1440]{2,1,0:T(8,128)(2,1)}, bf16[6,32,1440]{2,1,0:T(8,128)(2,1)}, bf16[32,24,256]{2,1,0:T(8,128)(2,1)}) custom-call(bf16[24,32,1440]{2,1,0:T(8,128)(2,1)} %fusion.3.rows_ref, bf16[32,24,256]{2,1,0:T(8,128)(2,1)} %bitcast.52), custom_call_target="tpu_custom_call" | custom-call | tf_op jit(solution)/shard_map/opening_exchange/pallas_call | solution.py:837
  45.1 0.0 all-gather.3.cloned.1.call-update
  45.2 0.1 ge.36
  45.3 0.1 ge.38
  45.4 0.1 reshape.111
  45.5 0.1 concatenate.24
  45.6 0.6 dynamic_slice.10.first_ref
  46.3 0.1 copy.30
  46.4 0.1 copy.34
  46.5 0.1 copy.31
  46.5 0.1 copy.32
  46.7 0.1 copy.33
  46.8 0.1 select_n.47
  46.9 0.1 copy.35
  47.0 0.1 copy.36
  47.1 0.1 copy.37
  47.2 0.2 eq.32
  47.4 1.6 slice_add_fusion
  49.0 0.4 copy-done.12
  49.4 1.3 fusion.8
  50.7 0.3 copy-done.11
  51.0 1.3 fusion.7
  52.3 0.1 pad_maximum_fusion
  52.4 1.4 fusion.5.home_ref
  53.9 2.2 fusion.6
  56.1 57.1 %outbound_legendre.1 = (bf16[5120,128]{1,0:T(8,128)(2,1)}, bf16[12,2,384,416]{3,2,1,0:T(8,128)(2,1)}, bf16[1536,768]{1,0:T(8,128)(2,1)}, bf16[1536,768]{1,0:T(8,128)(2,1)}) custom-call(bf16[32,24,768]{2,1,0:T(8,128)(2,1)} %bitcast.54, s32[12]{0:T(128)} %dynamic_slice.10.first_ref, bf16[12,721,384]{2,1,0:T(8,128)(2,1)} %leg_ref.1, ...), custom_call_target="tpu_custom_call" | custom-call | tf_op jit(solution)/shard_map/outbound_legendre/pallas_call | solution.py:726
  113.3 7.1 %all-to-all-start = ((bf16[32,160,128]{2,1,0:T(8,128)(2,1)}), bf16[32,160,128]{2,1,0:T(8,128)(2,1)S(1)}, u32[]{:S(2)}, u32[]{:S(2)}) async-start(bf16[32,160,128]{2,1,0:T(8,128)(2,1)} %bitcast.53), calls=%async_computation | async-start | bytes 2621440 | tf_op jit(solution)/shard_map/all_to_all | solution.py:913
  120.4 0.1 reshape.119
  120.5 0.1 broadcast_in_dim.54
  120.6 0.8 reshape.185.a_ref
  121.4 0.6 pad_add_fusion.place_ref
  122.0 5.4 %fusion.2 = bf16[1536,384]{0,1:T(8,128)(2,1)} fusion(bf16[384,1440]{1,0:T(8,128)(2,1)S(1)} %bitcast.57, bf16[1536,1440]{1,0:T(8,128)(2,1)} %constant.80.clone), kind=kOutput, calls=%fused_computation.5 | convolution fusion | flops 1699282944 | bytes 6709248 | tf_op jit(solution)/shard_map/dot_general | solution.py:868
  127.4 8.2 %unpack_weights.1 = bf16[24,4,8,8,256]{4,3,2,1,0:T(8,128)(2,1)} custom-call(bf16[8,32,24,256]{3,2,1,0:T(8,128)(2,1)} %bitcast.60, bf16[512,512]{1,0:T(8,128)(2,1)} %constant.79.clone.swap_ref), custom_call_target="tpu_custom_call" | custom-call | flops 4000000000 | bytes 6000000 | tf_op jit(solution)/shard_map/unpack_weights/pallas_call | solution.py:169
  135.6 3.9 %all-to-all-done.d_ref = bf16[32,160,128]{2,1,0:T(8,128)(2,1)S(1)} async-done(((bf16[32,160,128]{2,1,0:T(8,128)(2,1)}), bf16[32,160,128]{2,1,0:T(8,128)(2,1)S(1)}, u32[]{:S(2)}, u32[]{:S(2)}) %all-to-all-start) | async-done | bytes 1310752 | tf_op jit(solution)/shard_map/all_to_all | solution.py:913
  139.5 1.1 copy-done.3
  140.6 24.3 %mix_degrees.1 = bf16[32,160,128]{2,1,0:T(8,128)(2,1)} custom-call(s32[1]{0:T(128)} %bitcast.19.owner_ref, bf16[32,160,128]{2,1,0:T(8,128)(2,1)} %copy-done.3, bf16[24,256,256]{2,1,0:T(8,128)(2,1)} %bitcast.49, s32[128,1]{1,0:T(8,128)} %reshape.185.a_ref, bf16[512,512]{1,0:T(8,128)(2,1)} %constant.79.clone.swap_ref), custom_call_target="tpu_custom_call" | custom-call | tf_op jit(solution)/shard_map/mix_degrees/pallas_call | solution.py:280
  164.8 39.2 %legendre_inverse_home.1 = (bf16[12,64,721]{2,1,0:T(8,128)(2,1)}, bf16[3,32,8,768]{3,2,1,0:T(8,128)(2,1)}) custom-call(s32[12]{0:T(128)} %dynamic_slice.10.first_ref, bf16[5120,128]{1,0:T(8,128)(2,1)} %bitcast.47, bf16[12,2,384,416]{3,2,1,0:T(8,128)(2,1)} %get-tuple-element.25.turned_ref, bf16[512,512]{1,0:T(8,128)(2,1)} %constant.79.clone.swap_ref), custom_call_target="tpu_custom_call" | custom-call | tf_op jit(solution)/shard_map/legendre_inverse_home/pallas_call | solution.py:403
  204.1 2.3 fusion.11
  206.4 0.1 copy-done.13
  206.6 1.2 fusion.1
  207.7 1.4 copy.41
  209.1 32.0 %pointwise_tail.1 = (bf16[12,180,256]{2,1,0:T(8,128)(2,1)}, bf16[6,180,256]{2,1,0:T(8,128)(2,1)}, bf16[6,180,256]{2,1,0:T(8,128)(2,1)}) custom-call(bf16[8,192,384]{2,1,0:T(8,128)(2,1)} %bitcast.48, bf16[256,512]{1,0:T(8,128)(2,1)} %w_in_ref.1, bf16[512,256]{1,0:T(8,128)(2,1)} %w_out_ref.1, bf16[512,512]{1,0:T(8,128)(2,1)} %constant.79.clone.swap_ref), custom_call_target="tpu_custom_call" | custom-call | tf_op jit(solution)/shard_map/pointwise_tail/pallas_call | solution.py:541
  241.2 4.2 %assemble_bands.1 = bf16[4320,256]{1,0:T(8,128)(2,1)} custom-call(s32[2]{0:T(128)} %pad_add_fusion.place_ref, bf16[6,180,256]{2,1,0:T(8,128)(2,1)} %get-tuple-element.28.left_ref, bf16[12,180,256]{2,1,0:T(8,128)(2,1)} %get-tuple-element.29.own_ref, bf16[6,180,256]{2,1,0:T(8,128)(2,1)} %get-tuple-element.30.right_ref), custom_call_target="tpu_custom_call" | custom-call | tf_op jit(solution)/shard_map/assemble_bands/pallas_call | solution.py:586
  245.4 1.0 copy.45
  (34 shorter events, 0.2 us)
Async XLA Ops:
  7.2 2.7 %copy-start = (bf16[720,8,32]{0,2,1:T(8,128)(2,1)S(1)}, bf16[720,8,32]{0,2,1:T(8,128)(2,1)}, u32[]{:S(2)}) copy-start(bf16[720,8,32]{0,2,1:T(8,128)(2,1)} %param.22) | copy-start | bytes 1105924
  7.2 120.2 %all-gather.3.cloned.1.call-start = ((), (), s32[]{:S(2)}) async-start(), calls=%async_computation.1 | async-start | bytes 3538944 | tf_op jit(solution)/shard_map/all_gather | solution.py:893
  15.7 29.5 %copy-start.7 = (s32[384]{0:T(512)S(1)}, s32[384]{0:T(512)}, u32[]{:S(2)}) copy-start(s32[384]{0:T(512)} %param.19) | copy-start | bytes 4612
  15.7 31.7 %copy-start.2 = (bf16[24,32,1440]{2,1,0:T(8,128)(2,1)S(1)}, bf16[24,32,1440]{2,1,0:T(8,128)(2,1)}, u32[]{:S(2)}) copy-start(bf16[24,32,1440]{2,1,0:T(8,128)(2,1)} %fusion.3.rows_ref) | copy-start | bytes 6635524
  47.4 2.0 copy-start.12
  49.0 1.7 copy-start.4
  49.4 1.6 copy-start.11
  113.2 8.8 %copy-start.5 = (bf16[12,32,1440]{2,1,0:T(8,128)(2,1)S(1)}, bf16[12,32,1440]{2,1,0:T(8,128)(2,1)}, u32[]{:S(2)}) copy-start(bf16[12,32,1440]{2,1,0:T(8,128)(2,1)} %copy-done.4) | copy-start | bytes 3317764
  113.3 26.3 %all-to-all-start = ((bf16[32,160,128]{2,1,0:T(8,128)(2,1)}), bf16[32,160,128]{2,1,0:T(8,128)(2,1)S(1)}, u32[]{:S(2)}, u32[]{:S(2)}) async-start(bf16[32,160,128]{2,1,0:T(8,128)(2,1)} %bitcast.53), calls=%async_computation | async-start | bytes 2621440 | tf_op jit(solution)/shard_map/all_to_all | solution.py:913
  139.5 1.1 copy-start.3
  164.8 39.2 %copy-start.9 = (bf16[1536,768]{1,0:T(8,128)(2,1)S(1)}, bf16[1536,768]{1,0:T(8,128)(2,1)}, u32[]{:S(2)}) copy-start(bf16[1536,768]{1,0:T(8,128)(2,1)} %get-tuple-element.22) | copy-start | bytes 7077892
  204.0 2.4 copy-start.8
  204.1 2.4 copy-start.10
  204.1 2.5 copy-start.13
  241.2 4.3 %copy-start.6 = (bf16[12,64,721]{2,1,0:T(8,128)(2,1)S(1)}, bf16[12,64,721]{2,1,0:T(8,128)(2,1)}, u32[]{:S(2)}) copy-start(bf16[12,64,721]{2,1,0:T(8,128)(2,1)} %get-tuple-element.31) | copy-start | bytes 3322372
  241.2 5.3 %copy-start.1 = (bf16[720,8,32]{0,2,1:T(8,128)(2,1)S(1)}, bf16[720,8,32]{0,2,1:T(8,128)(2,1)}, u32[]{:S(2)}) copy-start(bf16[720,8,32]{0,2,1:T(8,128)(2,1)} %param.22) | copy-start | bytes 1105924
Sparse Core Ops, SparseCore 0:
  45.3 66.4 all-gather.2
